TPU v7x, 512 devices: a whole 4x4x16 slice. The times are simulated.
512 devices in a mesh: ctx: 64 (over x, z), head: 8 (over y, core).
Axes of the slice: x: 4, y: 4, z: 16, core: 2. Of those that a mesh axis runs over, the one named last changes fastest.
Arguments:
- queries: bfloat16 [32768, 4096], P('ctx', 'head'), may hold values from -6 to 6
- keys: bfloat16 [32768, 4096], P('ctx', 'head'), may hold values from -6 to 6
- values: bfloat16 [32768, 4096], P('ctx', 'head'), may hold values from -6 to 6
- out_weight: bfloat16 [4096, 4096], P('head', 'ctx'), may hold values from -0.25 to 0.25
Outputs:
- mixed: bfloat16 [32768, 4096], P('ctx', 'head')
All inputs are finite; a program needn't handle non-finite values.
Results may differ from a plain program's by a relative error of at most 0.024.
Values may be sent and summed in bfloat16 or wider, within the bound.
No kernel may reach another device: no remote copies, remote signals or barrier semaphores. Data moves between devices by JAX's collectives and lax.ppermute only.
A program may use at most 64 MiB of HBM per device.

v0:
```python
import jax
import jax.numpy as jnp
from jax import lax
from jax.sharding import PartitionSpec as P

HEAD_DIM = 128


def prefix_2(shard, axis, join, neutral):
    place = lax.axis_index(axis)
    gathered = lax.all_gather(shard.astype(jnp.bfloat16), axis)
    state = jnp.zeros_like(shard) + jnp.asarray(neutral, shard.dtype)

    def one(hop, state):
        return join(state, lax.dynamic_index_in_dim(gathered, hop, 0, False).astype(shard.dtype))

    return lax.fori_loop(0, place, one, state)


def add_states(earlier, later):
    return earlier + later


def local(queries, keys, values, out_weight):
    tok_rows = queries.shape[0]
    local_width = queries.shape[1]
    local_heads = local_width // HEAD_DIM
    q_heads = queries.reshape(tok_rows, local_heads, HEAD_DIM)
    k_heads = keys.reshape(tok_rows, local_heads, HEAD_DIM)
    v_heads = values.reshape(tok_rows, local_heads, HEAD_DIM)
    states = jnp.einsum("thd,the->hde", k_heads, v_heads, preferred_element_type=jnp.float32)
    prefix = prefix_2(states, "ctx", add_states, jnp.zeros_like(states))
    scores = jnp.einsum("thd,shd->hts", q_heads, k_heads, preferred_element_type=jnp.float32)
    causal = jnp.arange(tok_rows)[:, None] >= jnp.arange(tok_rows)[None, :]
    scores = jnp.where(causal[None], scores, jnp.float32(0.0)).astype(jnp.bfloat16)
    intra = jnp.einsum("hts,she->the", scores, v_heads, preferred_element_type=jnp.float32)
    inter = jnp.einsum(
        "thd,hde->the", q_heads, prefix.astype(jnp.bfloat16), preferred_element_type=jnp.float32
    )
    attn = inter + intra
    scale = lax.rsqrt(jnp.mean(attn * attn, axis=-1, keepdims=True) + 1e-06)
    hidden = (attn * scale).astype(jnp.bfloat16).reshape(tok_rows, local_width)
    terms = jnp.dot(
        hidden,
        lax.all_gather(out_weight, "ctx", axis=1, tiled=True),
        preferred_element_type=jnp.float32,
    )
    mixed = lax.psum_scatter(terms.astype(jnp.bfloat16), "head", scatter_dimension=1, tiled=True)
    return mixed


def solution(mesh):
    in_specs = (P("ctx", "head"), P("ctx", "head"), P("ctx", "head"), P("head", "ctx"))
    out_specs = P("ctx", "head")
    return jax.shard_map(local, mesh=mesh, in_specs=in_specs, out_specs=out_specs, check_vma=False)
```

profile of v0, /device:TPU:1, one launch (start us, length us, event | category | flops | bytes accessed | tf_op | source)
XLA Modules:
  0.0 368.4 jit_solution(10615070763231003769)
XLA Ops:
  6.5 0.0 copy-start
  6.5 0.0 all-gather.6.cloned.1.call-start
  6.5 1.3 copy.16
  7.9 1.3 copy.17
  9.1 1.0 convolution_convert_fusion.1
  10.1 0.0 all-gather.6.cloned.1.call-update
  10.1 0.0 all-gather.4.cloned.1.call-start
  10.1 0.7 all-gather.4.cloned.1.call-update
  10.8 0.0 reduce-scatter.2.cloned.1.call-start
  10.9 0.1 iota_compare_fusion
  11.0 153.7 %all-gather.6.cloned.1.call-done = bf16[256,128,128]{2,1,0:T(8,128)(2,1)} async-done(((bf16[4,128,128]{2,1,0:T(8,128)(2,1)}), bf16[256,128,128]{2,1,0:T(8,128)(2,1)}) %all-gather.6.cloned.1.call-update) | async-done | bytes 8388624 | tf_op jit(solution)/shard_map/all_gather | solution.py:11
  164.7 0.0 copy-done
  164.7 0.3 convolution_bitcast_fusion
  165.1 2.3 multiply_reduce_fusion
  167.4 1.4 multiply_convert_fusion
  168.7 140.4 %all-gather.4.cloned.1.call-done = bf16[512,4096]{0,1:T(8,128)(2,1)} async-done(((bf16[512,64]{0,1:T(8,128)(2,1)}), bf16[512,4096]{0,1:T(8,128)(2,1)}) %all-gather.4.cloned.1.call-update) | async-done | bytes 4194320 | tf_op jit(solution)/shard_map/all_gather | solution.py:45
  309.1 6.5 %convolution_convert_fusion = bf16[512,4096]{1,0:T(8,128)(2,1)} fusion(bf16[512,512]{0,1:T(8,128)(2,1)S(1)} %bitcast.41, bf16[512,4096]{0,1:T(8,128)(2,1)} %all-gather.4.cloned.1.call-done), kind=kOutput, calls=%fused_computation.1 | convolution fusion | flops 2149580800 | bytes 8912896 | tf_op jit(solution)/shard_map/dot_general | solution.py:43
  315.6 0.0 reduce-scatter.2.cloned.1.call-update
  315.7 46.2 %reduce-scatter.2.cloned.1.call-done = bf16[512,512]{1,0:T(8,128)(2,1)} async-done(((bf16[512,4096]{1,0:T(8,128)(2,1)}), bf16[512,512]{1,0:T(8,128)(2,1)}) %reduce-scatter.2.cloned.1.call-update) | async-done | bytes 524304 | tf_op jit(solution)/shard_map/reduce_scatter | solution.py:48
  (3 shorter events, 0.0 us)
Async XLA Ops:
  6.5 158.2 %copy-start = (bf16[512,512]{1,0:T(8,128)(2,1)S(1)}, bf16[512,512]{1,0:T(8,128)(2,1)}, u32[]{:S(2)}) copy-start(bf16[512,512]{1,0:T(8,128)(2,1)} %param.6) | copy-start | bytes 1572868
  6.5 158.1 %all-gather.6.cloned.1.call-start = ((), (), s32[]{:S(2)}) async-start(), calls=%async_computation.3 | async-start | bytes 8519680 | tf_op jit(solution)/shard_map/all_gather | solution.py:11
  10.1 299.0 %all-gather.4.cloned.1.call-start = ((), (), s32[]{:S(2)}) async-start(), calls=%async_computation.1 | async-start | bytes 4259840 | tf_op jit(solution)/shard_map/all_gather | solution.py:45
  10.8 351.0 %reduce-scatter.2.cloned.1.call-start = ((), (), s32[]{:S(2)}) async-start(), calls=%async_computation.2 | async-start | bytes 4718592 | tf_op jit(solution)/shard_map/reduce_scatter | solution.py:48
Sparse Core Ops, SparseCore 0:
  10.3 154.3 all-gather.5
  167.6 141.4 all-gather.3
  315.8 46.0 reduce-scatter.1
where the time goes:
time: 371 us; the launch traced here: 368 us
  waiting for transfers between devices  341 us (92%)
  between operations  13.2 us (4%)
  matrix products  10.1 us (3%)
    all_gather x1, waiting for transfers between devices, prefix_2(): gathered = lax.all_gather(shard.astype(jnp.bfloat16), axis)  154 us
    all_gather x1, waiting for transfers between devices, local(): lax.all_gather(out_weight, 'ctx', axis=1, tiled=True)  140 us
    reduce_scatter x1, waiting for transfers between devices, local(): lax.psum_scatter(terms.astype(jnp.bfloat16), 'head', scatter_dimension=1,...  46.2 us
  transfers between devices with their start and end apart: 3, of which 3 were waited for; matrix products, arithmetic and copies ran while one was open for 1% of the time, Pallas kernels for 0%

commit v1 on v0

v1 whole, which is shorter than its diff:
```python
import jax
import jax.numpy as jnp
from jax import lax
from jax.experimental import pallas as pl
from jax.experimental.pallas import tpu as pltpu
from jax.sharding import Mesh, PartitionSpec as P

HEAD_DIM = 128
NX, NZ, NY, NC = 4, 16, 4, 2
N_CTX = NX * NZ
BF = jnp.bfloat16
F32 = jnp.float32
VMEM = 48 * 1024 * 1024


def params():
    return pltpu.CompilerParams(vmem_limit_bytes=VMEM)


def whole(n):
    return [pl.BlockSpec(memory_space=pltpu.VMEM)] * n


def states_kernel(k_ref, v_ref, o_ref):
    for h in range(k_ref.shape[1] // HEAD_DIM):
        cols = slice(h * HEAD_DIM, (h + 1) * HEAD_DIM)
        o_ref[cols, :] = lax.dot_general(
            k_ref[:, cols], v_ref[:, cols], (((0,), (0,)), ((), ())), preferred_element_type=F32
        ).astype(BF)


def scan_kernel(s_ref, o_ref):
    total = jnp.zeros(s_ref.shape[1:], F32)
    for c in range(s_ref.shape[0]):
        o_ref[c] = total.astype(BF)
        total = total + s_ref[c].astype(F32)


def attention_kernel(q_ref, k_ref, v_ref, p_ref, o_ref):
    rows = q_ref.shape[0]
    blk = 256
    t = lax.broadcasted_iota(jnp.int32, (blk, blk), 0)
    s = lax.broadcasted_iota(jnp.int32, (blk, blk), 1)
    causal = t >= s
    for h in range(q_ref.shape[1] // HEAD_DIM):
        cols = slice(h * HEAD_DIM, (h + 1) * HEAD_DIM)
        prefix = p_ref[cols, :]
        for i in range(rows // blk):
            here = slice(i * blk, (i + 1) * blk)
            q = q_ref[here, cols]
            attn = jnp.dot(q, prefix, preferred_element_type=F32)
            for j in range(i + 1):
                there = slice(j * blk, (j + 1) * blk)
                scores = lax.dot_general(
                    q, k_ref[there, cols], (((1,), (1,)), ((), ())), preferred_element_type=F32
                )
                if i == j:
                    scores = jnp.where(causal, scores, 0.0)
                attn += jnp.dot(scores.astype(BF), v_ref[there, cols], preferred_element_type=F32)
            scale = lax.rsqrt(jnp.mean(attn * attn, axis=-1, keepdims=True) + 1e-06)
            o_ref[here, cols] = (attn * scale).astype(BF)


def projection_kernel(order_ref, *refs):
    hidden, (w_ref, o_ref) = refs[:8], refs[8:]
    zl = NZ // NC
    total = None
    for n, h_ref in enumerate(hidden):
        core, slot = order_ref[2 * n], order_ref[2 * n + 1]
        w = w_ref[pl.ds(core * zl, zl), slot].reshape(zl * w_ref.shape[2], w_ref.shape[3])
        part = lax.dot_general(h_ref[...], w, (((1,), (1,)), ((), ())), preferred_element_type=F32)
        total = part if total is None else total + part
    o_ref[...] = total.astype(BF)


def linear(x, z, y, c):
    return ((x * NZ + z) * NY + y) * NC + c


AXES = ("x", "z", "y", "c")


def weight_pairs(k):
    zl = NZ // NC
    pairs = []
    for x in range(NX):
        for z in range(NZ):
            for y in range(NY):
                for c in range(NC):
                    pairs.append(
                        (linear(x, z, y, c), linear((y + k) % NX, c * zl + z % zl, x, z // zl))
                    )
    return pairs


def local(queries, keys, values, out_weight):
    rows, width = queries.shape
    w = out_weight.T
    w4 = jnp.stack([lax.ppermute(w, AXES, weight_pairs(k)) for k in range(NX)])
    states = pl.pallas_call(
        states_kernel,
        out_shape=jax.ShapeDtypeStruct((width, HEAD_DIM), BF),
        in_specs=whole(2), out_specs=whole(1)[0], compiler_params=params(),
    )(keys, values)
    states, w4 = lax.optimization_barrier((states, w4))
    w_all = lax.all_gather(w4, "z")
    part = width // N_CTX
    mine = lax.all_to_all(states.reshape(N_CTX, part, HEAD_DIM), ("x", "z"), 0, 0)
    scanned = pl.pallas_call(
        scan_kernel,
        out_shape=jax.ShapeDtypeStruct(mine.shape, BF),
        in_specs=whole(1), out_specs=whole(1)[0], compiler_params=params(),
    )(mine)
    prefix = lax.all_to_all(scanned, ("x", "z"), 0, 0).reshape(width, HEAD_DIM)
    hidden = pl.pallas_call(
        attention_kernel,
        out_shape=jax.ShapeDtypeStruct((rows, width), BF),
        in_specs=whole(4), out_specs=whole(1)[0], compiler_params=params(),
    )(queries, keys, values, prefix)

    def along(axis, n, d, a):
        return lax.ppermute(a, axis, [(i, (i + d) % n) for i in range(n)])

    blocks = [hidden] + [along("y", NY, d, hidden) for d in (1, 3, 2)]
    others = [along("c", NC, 1, b) for b in blocks]
    me_x, me_y, me_c = lax.axis_index("x"), lax.axis_index("y"), lax.axis_index("c")
    order = []
    for flip in (0, 1):
        for d in (0, 1, 3, 2):
            source_y = (me_y - d) % NY
            order += [(me_c + flip) % NC, (me_x - source_y) % NX]
    order = jnp.stack(order).astype(jnp.int32)
    return pl.pallas_call(
        projection_kernel,
        out_shape=jax.ShapeDtypeStruct((rows, width), BF),
        in_specs=[pl.BlockSpec(memory_space=pltpu.SMEM)] + whole(9),
        out_specs=whole(1)[0], compiler_params=params(),
    )(order, *blocks, *others, w_all)


def solution(mesh):
    fine = Mesh(mesh.devices.reshape(NX, NZ, NY, NC), AXES)
    ctx, head = ("x", "z"), ("y", "c")
    in_specs = (P(ctx, head), P(ctx, head), P(ctx, head), P(head, ctx))
    return jax.shard_map(local, mesh=fine, in_specs=in_specs, out_specs=P(ctx, head), check_vma=False)
```

time: 371 us -> 160 us (0.43)
  waiting for transfers between devices: 341 us -> 18.5 us
  starting transfers between devices: 0.08 us -> 61.8 us
  blocking collectives: 0 us -> 49.8 us
  matrix products: 10.1 us -> 0 us
  Pallas kernels: 0 us -> 8.14 us
    all_gather x2 -> x1, waiting for transfers between devices: 294 us -> 0.01 us  [local(): w_all = lax.all_gather(w4, 'z')]
    ppermute x0 -> x11, starting transfers between devices: none -> 61.8 us  [the longest x4 38.7 us: local(): w4 = jnp.stack([lax.ppermute(w, AXES, weight_pairs(k)) for k in range(NX)])]
    all_to_all x0 -> x2, blocking collectives: none -> 49.8 us  [the longest x1 27.4 us: local(): lax.all_to_all(states.reshape(N_CTX, part, HEAD_DIM), ('x', 'z'), 0, 0)]
    reduce_scatter x1 -> x0, waiting for transfers between devices: 46.2 us -> none  [local(): lax.psum_scatter(terms.astype(jnp.bfloat16), 'head', scatter_dimension=1,...]
    ppermute x0 -> x11, waiting for transfers between devices: none -> 18.5 us  [the longest x7 9.59 us: along(): return lax.ppermute(a, axis, [(i, (i + d) % n) for i in range(n)])]
    dot_general x4 -> x0, matrix products: 10.1 us -> none  [the longest x1 6.53 us: local(): jnp.dot(hidden, lax.all_gather(out_weight, 'ctx', axis=1, tiled=True), pr...]
    pallas_call x0 -> x4, Pallas kernels: none -> 8.14 us  [the longest x1 5.68 us: local(): pl.pallas_call(projection_kernel, out_shape=jax.ShapeDtypeStruct((rows, w...]
    unnamed x2 -> x10, local copies, waits for them, and re-layouts: 0.01 us -> 5.21 us
  transfers between devices with their start and end apart: 3 -> 12, of which waited for: 3 -> 4; matrix products, arithmetic and copies ran while one was open for 1% -> 0% of each run, Pallas kernels for 0% -> 2%
where the time goes in v1:
time: 160 us; the launch traced here: 158 us
  starting transfers between devices  61.8 us (39%)
  blocking collectives  49.8 us (31%)
  waiting for transfers between devices  18.5 us (12%)
  between operations  13.7 us (9%)
  Pallas kernels  8.14 us (5%)
  local copies, waits for them, and re-layouts  5.3 us (3%)
    ppermute x4, starting transfers between devices, local(): w4 = jnp.stack([lax.ppermute(w, AXES, weight_pairs(k)) for k in range(NX)])  38.7 us
    all_to_all x1, blocking collectives, local(): lax.all_to_all(states.reshape(N_CTX, part, HEAD_DIM), ('x', 'z'), 0, 0)  27.4 us
    ppermute x7, starting transfers between devices, along(): return lax.ppermute(a, axis, [(i, (i + d) % n) for i in range(n)])  23 us
    all_to_all x1, blocking collectives, local(): prefix = lax.all_to_all(scanned, ('x', 'z'), 0, 0).reshape(width, HEAD_DIM)  22.4 us
    ppermute x7, waiting for transfers between devices, along(): return lax.ppermute(a, axis, [(i, (i + d) % n) for i in range(n)])  9.59 us
    ppermute x4, waiting for transfers between devices, local(): w4 = jnp.stack([lax.ppermute(w, AXES, weight_pairs(k)) for k in range(NX)])  8.92 us
    pallas_call x1, Pallas kernels, local(): pl.pallas_call(projection_kernel, out_shape=jax.ShapeDtypeStruct((rows, w...  5.68 us
    unnamed x10, local copies, waits for them, and re-layouts  5.21 us
  transfers between devices with their start and end apart: 12, of which 4 were waited for; matrix products, arithmetic and copies ran while one was open for 0% of the time, Pallas kernels for 2%

profile of v1, /device:TPU:1, one launch (start us, length us, event | category | flops | bytes accessed | tf_op | source)
XLA Modules:
  0.0 158.0 jit_solution(14796938270950876001)
XLA Ops:
  6.5 0.0 all-gather.3.cloned.1.call-start
  6.5 19.0 %collective-permute-start.3 = (bf16[64,512]{1,0:T(8,128)(2,1)}, bf16[64,512]{1,0:T(8,128)(2,1)S(1)}, u32[]{:S(2)}, u32[]{:S(2)}) collective-permute-start(bf16[64,512]{1,0:T(8,128)(2,1)} %bitcast.21), channel_id=1, source_target_pairs={{0,384},{1,448},{2,0},{3,64},{4,128},{5,192},{6,256},{7,320},{8,39... | collective-permute-start | bytes 196616 | tf_op jit(solution)/shard_map/ppermute | solution.py:99
  25.6 2.2 %collective-permute-start.2 = (bf16[64,512]{1,0:T(8,128)(2,1)}, bf16[64,512]{1,0:T(8,128)(2,1)S(1)}, u32[]{:S(2)}, u32[]{:S(2)}) collective-permute-start(bf16[64,512]{1,0:T(8,128)(2,1)} %bitcast.22), channel_id=1, source_target_pairs={{0,256},{1,320},{2,384},{3,448},{4,0},{5,64},{6,128},{7,192},{8,26... | collective-permute-start | bytes 196616 | tf_op jit(solution)/shard_map/ppermute | solution.py:99
  27.8 13.7 %collective-permute-start.1 = (bf16[64,512]{1,0:T(8,128)(2,1)}, bf16[64,512]{1,0:T(8,128)(2,1)S(1)}, u32[]{:S(2)}, u32[]{:S(2)}) collective-permute-start(bf16[64,512]{1,0:T(8,128)(2,1)} %bitcast.23), channel_id=1, source_target_pairs={{0,128},{1,192},{2,256},{3,320},{4,384},{5,448},{6,0},{7,64},{8,13... | collective-permute-start | bytes 196616 | tf_op jit(solution)/shard_map/ppermute | solution.py:99
  41.5 3.8 %collective-permute-start = (bf16[64,512]{1,0:T(8,128)(2,1)}, bf16[64,512]{1,0:T(8,128)(2,1)S(1)}, u32[]{:S(2)}, u32[]{:S(2)}) collective-permute-start(bf16[64,512]{1,0:T(8,128)(2,1)} %bitcast.24), channel_id=1, source_target_pairs={{0,0},{1,64},{2,128},{3,192},{4,256},{5,320},{6,384},{7,448},{8,8}... | collective-permute-start | bytes 196616 | tf_op jit(solution)/shard_map/ppermute | solution.py:99
  45.3 0.0 copy-start
  45.3 1.0 copy-done
  46.4 0.0 copy-start.2
  46.4 1.0 copy-done.2
  47.4 0.3 shard_map.46
  47.7 0.0 collective-permute-done.3
  47.8 0.0 collective-permute-done.2
  47.8 0.0 collective-permute-done.1
  47.8 8.9 %collective-permute-done = bf16[64,512]{1,0:T(8,128)(2,1)S(1)} collective-permute-done((bf16[64,512]{1,0:T(8,128)(2,1)}, bf16[64,512]{1,0:T(8,128)(2,1)S(1)}, u32[]{:S(2)}, u32[]{:S(2)}) %collective-permute-start) | collective-permute-done | bytes 65568 | tf_op jit(solution)/shard_map/ppermute | solution.py:99
  56.7 0.7 pad_maximum_fusion
  57.4 0.0 all-gather.3.cloned.1.call-update
  57.5 27.4 %all_to_all.10.s_ref = bf16[64,8,128]{2,1,0:T(8,128)(2,1)S(1)} all-to-all(bf16[64,8,128]{2,1,0:T(8,128)(2,1)S(1)} %bitcast.14), channel_id=1, replica_groups=mesh['x'=4,'z'=16,'y'=4,'c'=2] {'x','z'}, dimensions={0} | all-to-all | bytes 262144 | tf_op jit(solution)/shard_map/all_to_all | solution.py:108
  84.8 0.1 shard_map.47
  84.9 22.4 %all_to_all.11 = bf16[64,8,128]{2,1,0:T(8,128)(2,1)S(1)} all-to-all(bf16[64,8,128]{2,1,0:T(8,128)(2,1)S(1)} %shard_map.47), channel_id=1, replica_groups=mesh['x'=4,'z'=16,'y'=4,'c'=2] {'x','z'}, dimensions={0} | all-to-all | bytes 262144 | tf_op jit(solution)/shard_map/all_to_all | solution.py:114
  107.3 0.0 copy-start.1
  107.3 1.0 copy-done.1
  108.3 0.0 copy-start.3
  108.3 1.0 copy-done.3
  109.4 0.0 copy-start.4
  109.4 1.0 copy-done.4
  110.4 2.0 %shard_map.48.refs_0_ = bf16[512,512]{1,0:T(8,128)(2,1)S(1)} custom-call(bf16[512,512]{1,0:T(8,128)(2,1)S(1)} %copy-done.4, bf16[512,512]{1,0:T(8,128)(2,1)S(1)} %copy-done.1, bf16[512,512]{1,0:T(8,128)(2,1)S(1)} %copy-done.3, bf16[512,128]{1,0:T(8,128)(2,1)S(1)} %bitcast.15), custom_call_target="tpu_custom_call" | custom-call | tf_op jit(solution)/shard_map/pallas_call | solution.py:115
  112.5 1.9 %collective-permute-start.6 = (bf16[512,512]{1,0:T(8,128)(2,1)S(1)}, bf16[512,512]{1,0:T(8,128)(2,1)S(1)}, u32[]{:S(2)}, u32[]{:S(2)}) collective-permute-start(bf16[512,512]{1,0:T(8,128)(2,1)S(1)} %shard_map.48.refs_0_), channel_id=1, source_target_pairs={{0,4},{2,6},{4,0},{6,2},{1,5},{3,7},{5,1},{7,3},{8,12},{10,14},{12... | collective-permute-start | bytes 1572872 | tf_op jit(solution)/shard_map/ppermute | solution.py:122
  114.4 5.3 %collective-permute-start.5 = (bf16[512,512]{1,0:T(8,128)(2,1)S(1)}, bf16[512,512]{1,0:T(8,128)(2,1)S(1)}, u32[]{:S(2)}, u32[]{:S(2)}) collective-permute-start(bf16[512,512]{1,0:T(8,128)(2,1)S(1)} %shard_map.48.refs_0_), channel_id=1, source_target_pairs={{0,6},{2,0},{4,2},{6,4},{1,7},{3,1},{5,3},{7,5},{8,14},{10,8},{12,... | collective-permute-start | bytes 1572872 | tf_op jit(solution)/shard_map/ppermute | solution.py:122
  119.7 1.9 %collective-permute-start.4 = (bf16[512,512]{1,0:T(8,128)(2,1)S(1)}, bf16[512,512]{1,0:T(8,128)(2,1)S(1)}, u32[]{:S(2)}, u32[]{:S(2)}) collective-permute-start(bf16[512,512]{1,0:T(8,128)(2,1)S(1)} %shard_map.48.refs_0_), channel_id=1, source_target_pairs={{0,2},{2,4},{4,6},{6,0},{1,3},{3,5},{5,7},{7,1},{8,10},{10,12},{12... | collective-permute-start | bytes 1572872 | tf_op jit(solution)/shard_map/ppermute | solution.py:122
  121.7 2.9 %collective-permute-start.7 = (bf16[512,512]{1,0:T(8,128)(2,1)S(1)}, bf16[512,512]{1,0:T(8,128)(2,1)S(1)}, u32[]{:S(2)}, u32[]{:S(2)}) collective-permute-start(bf16[512,512]{1,0:T(8,128)(2,1)S(1)} %shard_map.48.refs_0_), channel_id=1, source_target_pairs={{0,1},{1,0},{2,3},{3,2},{4,5},{5,4},{6,7},{7,6},{8,9},{9,8},{10,11... | collective-permute-start | bytes 1572872 | tf_op jit(solution)/shard_map/ppermute | solution.py:122
  124.6 3.3 %collective-permute-done.6.refs_3_ = bf16[512,512]{1,0:T(8,128)(2,1)S(1)} collective-permute-done((bf16[512,512]{1,0:T(8,128)(2,1)S(1)}, bf16[512,512]{1,0:T(8,128)(2,1)S(1)}, u32[]{:S(2)}, u32[]{:S(2)}) %collective-permute-start.6) | collective-permute-done | bytes 524320 | tf_op jit(solution)/shard_map/ppermute | solution.py:122
  127.9 6.2 %collective-permute-start.10 = (bf16[512,512]{1,0:T(8,128)(2,1)S(1)}, bf16[512,512]{1,0:T(8,128)(2,1)S(1)}, u32[]{:S(2)}, u32[]{:S(2)}) collective-permute-start(bf16[512,512]{1,0:T(8,128)(2,1)S(1)} %collective-permute-done.6.refs_3_), channel_id=1, source_target_pairs={{0,1},{1,0},{2,3},{3,2},{4,5},{5,4},{6,7},{7,6},{8,9},{9,8},{10,11... | collective-permute-start | bytes 1572872 | tf_op jit(solution)/shard_map/ppermute | solution.py:122
  134.1 4.5 %collective-permute-done.5.refs_2_ = bf16[512,512]{1,0:T(8,128)(2,1)S(1)} collective-permute-done((bf16[512,512]{1,0:T(8,128)(2,1)S(1)}, bf16[512,512]{1,0:T(8,128)(2,1)S(1)}, u32[]{:S(2)}, u32[]{:S(2)}) %collective-permute-start.5) | collective-permute-done | bytes 524320 | tf_op jit(solution)/shard_map/ppermute | solution.py:122
  138.7 2.8 %collective-permute-start.9 = (bf16[512,512]{1,0:T(8,128)(2,1)S(1)}, bf16[512,512]{1,0:T(8,128)(2,1)}, u32[]{:S(2)}, u32[]{:S(2)}) collective-permute-start(bf16[512,512]{1,0:T(8,128)(2,1)S(1)} %collective-permute-done.5.refs_2_), channel_id=1, source_target_pairs={{0,1},{1,0},{2,3},{3,2},{4,5},{5,4},{6,7},{7,6},{8,9},{9,8},{10,11... | collective-permute-start | bytes 1572872 | tf_op jit(solution)/shard_map/ppermute | solution.py:122
  141.5 0.0 collective-permute-done.4.refs_1_
  141.5 1.9 %collective-permute-start.8 = (bf16[512,512]{1,0:T(8,128)(2,1)S(1)}, bf16[512,512]{1,0:T(8,128)(2,1)}, u32[]{:S(2)}, u32[]{:S(2)}) collective-permute-start(bf16[512,512]{1,0:T(8,128)(2,1)S(1)} %collective-permute-done.4.refs_1_), channel_id=1, source_target_pairs={{0,1},{1,0},{2,3},{3,2},{4,5},{5,4},{6,7},{7,6},{8,9},{9,8},{10,11... | collective-permute-start | bytes 1572872 | tf_op jit(solution)/shard_map/ppermute | solution.py:122
  143.5 0.1 stack.52.order_ref
  143.6 0.0 collective-permute-done.7.refs_4_
  143.7 0.0 collective-permute-done.10.refs_7_
  143.7 0.0 collective-permute-done.9.refs_6_
  143.7 1.7 %collective-permute-done.8.refs_5_ = bf16[512,512]{1,0:T(8,128)(2,1)} collective-permute-done((bf16[512,512]{1,0:T(8,128)(2,1)S(1)}, bf16[512,512]{1,0:T(8,128)(2,1)}, u32[]{:S(2)}, u32[]{:S(2)}) %collective-permute-start.8) | collective-permute-done | bytes 524320 | tf_op jit(solution)/shard_map/ppermute | solution.py:122
  145.4 0.0 all-gather.3.cloned.1.call-done
  145.4 5.7 %shard_map.49 = bf16[512,512]{1,0:T(8,128)(2,1)} custom-call(s32[16]{0:T(128)S(1)} %stack.52.order_ref, bf16[512,512]{1,0:T(8,128)(2,1)S(1)} %shard_map.48.refs_0_, bf16[512,512]{1,0:T(8,128)(2,1)S(1)} %collective-permute-done.4.refs_1_, bf16[512,512]{1,0:T(8,128)(2,1)S(1)} %collective-permute-done.5.refs_2_, ...), custom_call_target="tpu_custom_call" | custom-call | tf_op jit(solution)/shard_map/pallas_call | solution.py:133
Async XLA Ops:
  6.5 138.9 %all-gather.3.cloned.1.call-start = ((), (), s32[]{:S(2)}) async-start(), calls=%async_computation.2 | async-start | bytes 4456448 | tf_op jit(solution)/shard_map/all_gather | solution.py:106
  6.5 41.2 %collective-permute-start.3 = (bf16[64,512]{1,0:T(8,128)(2,1)}, bf16[64,512]{1,0:T(8,128)(2,1)S(1)}, u32[]{:S(2)}, u32[]{:S(2)}) collective-permute-start(bf16[64,512]{1,0:T(8,128)(2,1)} %bitcast.21), channel_id=1, source_target_pairs={{0,384},{1,448},{2,0},{3,64},{4,128},{5,192},{6,256},{7,320},{8,39... | collective-permute-start | bytes 196616 | tf_op jit(solution)/shard_map/ppermute | solution.py:99
  25.6 22.2 %collective-permute-start.2 = (bf16[64,512]{1,0:T(8,128)(2,1)}, bf16[64,512]{1,0:T(8,128)(2,1)S(1)}, u32[]{:S(2)}, u32[]{:S(2)}) collective-permute-start(bf16[64,512]{1,0:T(8,128)(2,1)} %bitcast.22), channel_id=1, source_target_pairs={{0,256},{1,320},{2,384},{3,448},{4,0},{5,64},{6,128},{7,192},{8,26... | collective-permute-start | bytes 196616 | tf_op jit(solution)/shard_map/ppermute | solution.py:99
  27.8 20.0 %collective-permute-start.1 = (bf16[64,512]{1,0:T(8,128)(2,1)}, bf16[64,512]{1,0:T(8,128)(2,1)S(1)}, u32[]{:S(2)}, u32[]{:S(2)}) collective-permute-start(bf16[64,512]{1,0:T(8,128)(2,1)} %bitcast.23), channel_id=1, source_target_pairs={{0,128},{1,192},{2,256},{3,320},{4,384},{5,448},{6,0},{7,64},{8,13... | collective-permute-start | bytes 196616 | tf_op jit(solution)/shard_map/ppermute | solution.py:99
  41.5 15.2 %collective-permute-start = (bf16[64,512]{1,0:T(8,128)(2,1)}, bf16[64,512]{1,0:T(8,128)(2,1)S(1)}, u32[]{:S(2)}, u32[]{:S(2)}) collective-permute-start(bf16[64,512]{1,0:T(8,128)(2,1)} %bitcast.24), channel_id=1, source_target_pairs={{0,0},{1,64},{2,128},{3,192},{4,256},{5,320},{6,384},{7,448},{8,8}... | collective-permute-start | bytes 196616 | tf_op jit(solution)/shard_map/ppermute | solution.py:99
  45.3 1.0 copy-start
  46.4 1.0 copy-start.2
  107.3 1.0 copy-start.1
  108.3 1.0 copy-start.3
  109.4 1.0 copy-start.4
  112.5 15.4 %collective-permute-start.6 = (bf16[512,512]{1,0:T(8,128)(2,1)S(1)}, bf16[512,512]{1,0:T(8,128)(2,1)S(1)}, u32[]{:S(2)}, u32[]{:S(2)}) collective-permute-start(bf16[512,512]{1,0:T(8,128)(2,1)S(1)} %shard_map.48.refs_0_), channel_id=1, source_target_pairs={{0,4},{2,6},{4,0},{6,2},{1,5},{3,7},{5,1},{7,3},{8,12},{10,14},{12... | collective-permute-start | bytes 1572872 | tf_op jit(solution)/shard_map/ppermute | solution.py:122
  114.4 24.3 %collective-permute-start.5 = (bf16[512,512]{1,0:T(8,128)(2,1)S(1)}, bf16[512,512]{1,0:T(8,128)(2,1)S(1)}, u32[]{:S(2)}, u32[]{:S(2)}) collective-permute-start(bf16[512,512]{1,0:T(8,128)(2,1)S(1)} %shard_map.48.refs_0_), channel_id=1, source_target_pairs={{0,6},{2,0},{4,2},{6,4},{1,7},{3,1},{5,3},{7,5},{8,14},{10,8},{12,... | collective-permute-start | bytes 1572872 | tf_op jit(solution)/shard_map/ppermute | solution.py:122
  119.7 21.7 %collective-permute-start.4 = (bf16[512,512]{1,0:T(8,128)(2,1)S(1)}, bf16[512,512]{1,0:T(8,128)(2,1)S(1)}, u32[]{:S(2)}, u32[]{:S(2)}) collective-permute-start(bf16[512,512]{1,0:T(8,128)(2,1)S(1)} %shard_map.48.refs_0_), channel_id=1, source_target_pairs={{0,2},{2,4},{4,6},{6,0},{1,3},{3,5},{5,7},{7,1},{8,10},{10,12},{12... | collective-permute-start | bytes 1572872 | tf_op jit(solution)/shard_map/ppermute | solution.py:122
  121.7 22.0 %collective-permute-start.7 = (bf16[512,512]{1,0:T(8,128)(2,1)S(1)}, bf16[512,512]{1,0:T(8,128)(2,1)S(1)}, u32[]{:S(2)}, u32[]{:S(2)}) collective-permute-start(bf16[512,512]{1,0:T(8,128)(2,1)S(1)} %shard_map.48.refs_0_), channel_id=1, source_target_pairs={{0,1},{1,0},{2,3},{3,2},{4,5},{5,4},{6,7},{7,6},{8,9},{9,8},{10,11... | collective-permute-start | bytes 1572872 | tf_op jit(solution)/shard_map/ppermute | solution.py:122
  127.9 15.7 %collective-permute-start.10 = (bf16[512,512]{1,0:T(8,128)(2,1)S(1)}, bf16[512,512]{1,0:T(8,128)(2,1)S(1)}, u32[]{:S(2)}, u32[]{:S(2)}) collective-permute-start(bf16[512,512]{1,0:T(8,128)(2,1)S(1)} %collective-permute-done.6.refs_3_), channel_id=1, source_target_pairs={{0,1},{1,0},{2,3},{3,2},{4,5},{5,4},{6,7},{7,6},{8,9},{9,8},{10,11... | collective-permute-start | bytes 1572872 | tf_op jit(solution)/shard_map/ppermute | solution.py:122
  138.7 5.0 %collective-permute-start.9 = (bf16[512,512]{1,0:T(8,128)(2,1)S(1)}, bf16[512,512]{1,0:T(8,128)(2,1)}, u32[]{:S(2)}, u32[]{:S(2)}) collective-permute-start(bf16[512,512]{1,0:T(8,128)(2,1)S(1)} %collective-permute-done.5.refs_2_), channel_id=1, source_target_pairs={{0,1},{1,0},{2,3},{3,2},{4,5},{5,4},{6,7},{7,6},{8,9},{9,8},{10,11... | collective-permute-start | bytes 1572872 | tf_op jit(solution)/shard_map/ppermute | solution.py:122
  141.5 3.9 %collective-permute-start.8 = (bf16[512,512]{1,0:T(8,128)(2,1)S(1)}, bf16[512,512]{1,0:T(8,128)(2,1)}, u32[]{:S(2)}, u32[]{:S(2)}) collective-permute-start(bf16[512,512]{1,0:T(8,128)(2,1)S(1)} %collective-permute-done.4.refs_1_), channel_id=1, source_target_pairs={{0,1},{1,0},{2,3},{3,2},{4,5},{5,4},{6,7},{7,6},{8,9},{9,8},{10,11... | collective-permute-start | bytes 1572872 | tf_op jit(solution)/shard_map/ppermute | solution.py:122
Sparse Core Ops, SparseCore 0:
  57.6 75.1 all-gather.2

commit v2 on v1

v2 whole, which is shorter than its diff:
```python
import jax
import jax.numpy as jnp
from jax import lax
from jax.experimental import pallas as pl
from jax.experimental.pallas import tpu as pltpu
from jax.sharding import Mesh, PartitionSpec as P

HEAD_DIM = 128
NX, NZ, NY, NC = 4, 16, 4, 2
N_CTX = NX * NZ
BF = jnp.bfloat16
F32 = jnp.float32


def params():
    return pltpu.CompilerParams(vmem_limit_bytes=48 * 1024 * 1024)


def states_kernel(k_ref, v_ref, o_ref):
    o_ref[...] = lax.dot_general(
        k_ref[...], v_ref[...], (((0,), (0,)), ((), ())), preferred_element_type=F32
    ).astype(BF)


def scan_kernel(s_ref, o_ref):
    total = jnp.zeros(s_ref.shape[1:], F32)
    for c in range(s_ref.shape[0]):
        o_ref[c] = total.astype(BF)
        total = total + s_ref[c].astype(F32)


def attention_kernel(q_ref, k_ref, v_ref, p_ref, o_ref):
    rows = q_ref.shape[0]
    blk = 256
    t = lax.broadcasted_iota(jnp.int32, (blk, blk), 0)
    s = lax.broadcasted_iota(jnp.int32, (blk, blk), 1)
    causal = t >= s
    prefix = p_ref[...]
    for i in range(rows // blk):
        here = slice(i * blk, (i + 1) * blk)
        q = q_ref[here, :]
        attn = jnp.dot(q, prefix, preferred_element_type=F32)
        for j in range(i + 1):
            there = slice(j * blk, (j + 1) * blk)
            scores = lax.dot_general(
                q, k_ref[there, :], (((1,), (1,)), ((), ())), preferred_element_type=F32
            )
            if i == j:
                scores = jnp.where(causal, scores, 0.0)
            attn += jnp.dot(scores.astype(BF), v_ref[there, :], preferred_element_type=F32)
        scale = lax.rsqrt(jnp.mean(attn * attn, axis=-1, keepdims=True) + 1e-06)
        hidden = (attn * scale).astype(BF)
        for n in range(o_ref.shape[0]):
            o_ref[n, here, :] = hidden


def projection_kernel(order_ref, h_ref, w_ref, o_ref):
    blocks, _, cols, depth = w_ref.shape
    total = None
    for y in range(h_ref.shape[0]):
        w = w_ref[:, order_ref[1 + y]].reshape(blocks * cols, depth)
        part = lax.dot_general(h_ref[y], w, (((1,), (1,)), ((), ())), preferred_element_type=F32)
        total = part if total is None else total + part
    o_ref[...] = total.astype(o_ref.dtype)


def add_kernel(a_ref, b_ref, o_ref):
    o_ref[...] = (a_ref[...] + b_ref[...].astype(F32)).astype(BF)


def project(order, hidden, w_all, dtype):
    sources, rows, depth = hidden.shape
    slots, cols = w_all.shape[1:3]
    zb = 4
    width = NZ // NC * cols
    steps = NZ // NC // zb
    return pl.pallas_call(
        projection_kernel,
        grid_spec=pltpu.PrefetchScalarGridSpec(
            num_scalar_prefetch=1,
            grid=(steps,),
            in_specs=[
                pl.BlockSpec((sources, rows, depth), lambda n, order: (0, 0, 0)),
                pl.BlockSpec((zb, slots, cols, depth), lambda n, order: (order[0] * steps + n, 0, 0, 0)),
            ],
            out_specs=pl.BlockSpec((rows, zb * cols), lambda n, order: (0, n)),
        ),
        out_shape=jax.ShapeDtypeStruct((rows, width), dtype),
        compiler_params=params(),
    )(order, hidden, w_all)


AXES = ("x", "z", "y", "c")


def local(queries, keys, values, out_weight):
    rows, width = queries.shape
    heads = width // HEAD_DIM
    me_x, me_c = lax.axis_index("x"), lax.axis_index("c")

    w = out_weight.T
    w4 = jnp.stack([
        lax.ppermute(
            w, ("x", "y"),
            [(x * NY + y, (y + k) % NX * NY + x) for x in range(NX) for y in range(NY)],
        )
        for k in range(NX)
    ])
    by_head = pl.BlockSpec((rows, HEAD_DIM), lambda h: (0, h))
    state = pl.BlockSpec((HEAD_DIM, HEAD_DIM), lambda h: (h, 0))
    states = pl.pallas_call(
        states_kernel,
        grid=(heads,),
        out_shape=jax.ShapeDtypeStruct((width, HEAD_DIM), BF),
        in_specs=[by_head, by_head], out_specs=state, compiler_params=params(),
    )(keys, values)
    states, w4 = lax.optimization_barrier((states, w4))
    w_all = lax.all_gather(w4, "z")
    part = width // N_CTX
    mine = lax.all_to_all(states.reshape(N_CTX, part, HEAD_DIM), ("x", "z"), 0, 0)
    scanned = pl.pallas_call(
        scan_kernel, out_shape=jax.ShapeDtypeStruct(mine.shape, BF), compiler_params=params(),
    )(mine)
    prefix = lax.all_to_all(scanned, ("x", "z"), 0, 0).reshape(width, HEAD_DIM)
    hidden = pl.pallas_call(
        attention_kernel,
        grid=(heads,),
        out_shape=jax.ShapeDtypeStruct((NY, rows, width), BF),
        in_specs=[by_head, by_head, by_head, state],
        out_specs=pl.BlockSpec((NY, rows, HEAD_DIM), lambda h: (0, 0, h)),
        compiler_params=params(),
    )(queries, keys, values, prefix)
    hidden = lax.all_to_all(hidden, "y", 0, 0)
    slots = [(me_x - y) % NX for y in range(NY)]
    away = jnp.stack([1 - me_c] + slots).astype(jnp.int32)
    home = jnp.stack([me_c] + slots).astype(jnp.int32)
    other = project(away, hidden, w_all, BF)
    other = lax.ppermute(other, "c", [(0, 1), (1, 0)])
    own = project(home, hidden, w_all, F32)
    tile = pl.BlockSpec((rows // 2, width), lambda n: (n, 0))
    return pl.pallas_call(
        add_kernel,
        grid=(2,),
        out_shape=jax.ShapeDtypeStruct((rows, width), BF),
        in_specs=[tile, tile], out_specs=tile, compiler_params=params(),
    )(own, other)


def solution(mesh):
    fine = Mesh(mesh.devices.reshape(NX, NZ, NY, NC), AXES)
    ctx, head = ("x", "z"), ("y", "c")
    in_specs = (P(ctx, head), P(ctx, head), P(ctx, head), P(head, ctx))
    return jax.shard_map(local, mesh=fine, in_specs=in_specs, out_specs=P(ctx, head), check_vma=False)
```

time: 160 us -> 135 us (0.84)
  starting transfers between devices: 61.8 us -> 30.1 us
  Pallas kernels: 8.14 us -> 12.2 us
  waiting for transfers between devices: 18.5 us -> 21.3 us
  blocking collectives: 49.8 us -> 51.9 us
    ppermute x11 -> x5, starting transfers between devices: 61.8 us -> 26.5 us  [the longest x4 17 us: local(): lax.ppermute(w, ('x', 'y'), [(x * NY + y, (y + k) % NX * NY + x) for x in...]
    all_to_all x0 -> x1, waiting for transfers between devices: none -> 19.8 us  [local(): hidden = lax.all_to_all(hidden, 'y', 0, 0)]
    ppermute x11 -> x5, waiting for transfers between devices: 18.5 us -> 0.01 us  [the longest x4 0.01 us: local(): lax.ppermute(w, ('x', 'y'), [(x * NY + y, (y + k) % NX * NY + x) for x in...]
    all_to_all x1, blocking collectives: 27.4 us -> 32.2 us  [local(): lax.all_to_all(states.reshape(N_CTX, part, HEAD_DIM), ('x', 'z'), 0, 0)]
    pallas_call x3 -> x5, Pallas kernels: 8.07 us -> 12.2 us  [the longest x2 6.65 us: project(): pl.pallas_call(projection_kernel, grid_spec=pltpu.PrefetchScalarGridSpec(...]
    all_to_all x0 -> x1, starting transfers between devices: none -> 3.61 us  [local(): hidden = lax.all_to_all(hidden, 'y', 0, 0)]
    all_to_all x1, blocking collectives: 22.4 us -> 19.7 us  [local(): prefix = lax.all_to_all(scanned, ('x', 'z'), 0, 0).reshape(width, HEAD_DIM)]
    unnamed x10 -> x12, local copies, waits for them, and re-layouts: 5.21 us -> 4.46 us
  transfers between devices with their start and end apart: 12 -> 7, of which waited for: 4 -> 2; matrix products, arithmetic and copies ran while one was open for 0% -> 0% of each run, Pallas kernels for 2% -> 6%
where the time goes in v2:
time: 135 us
  blocking collectives  51.9 us (38%)
  starting transfers between devices  30.1 us (22%)
  waiting for transfers between devices  21.3 us (16%)
  between operations  13.6 us (10%)
  Pallas kernels  12.2 us (9%)
  local copies, waits for them, and re-layouts  4.63 us (3%)
    all_to_all x1, blocking collectives, local(): lax.all_to_all(states.reshape(N_CTX, part, HEAD_DIM), ('x', 'z'), 0, 0)  32.2 us
    all_to_all x1, waiting for transfers between devices, local(): hidden = lax.all_to_all(hidden, 'y', 0, 0)  19.8 us
    all_to_all x1, blocking collectives, local(): prefix = lax.all_to_all(scanned, ('x', 'z'), 0, 0).reshape(width, HEAD_DIM)  19.7 us
    ppermute x4, starting transfers between devices, local(): lax.ppermute(w, ('x', 'y'), [(x * NY + y, (y + k) % NX * NY + x) for x in...  17 us
    ppermute x1, starting transfers between devices, local(): other = lax.ppermute(other, 'c', [(0, 1), (1, 0)])  9.44 us
    pallas_call x2, Pallas kernels, project(): pl.pallas_call(projection_kernel, grid_spec=pltpu.PrefetchScalarGridSpec(...  6.65 us
    unnamed x12, local copies, waits for them, and re-layouts  4.46 us
    all_to_all x1, starting transfers between devices, local(): hidden = lax.all_to_all(hidden, 'y', 0, 0)  3.61 us
  transfers between devices with their start and end apart: 7, of which 2 were waited for; matrix products, arithmetic and copies ran while one was open for 0% of the time, Pallas kernels for 6%

profile of v2, /device:TPU:1, one launch (start us, length us, event | category | flops | bytes accessed | tf_op | source)
XLA Modules:
  0.0 134.5 jit_solution(18251440070659884030)
XLA Ops:
  6.5 0.0 all-gather.3.cloned.1.call-start
  6.5 1.5 %collective-permute-start = (bf16[64,512]{1,0:T(8,128)(2,1)}, bf16[64,512]{1,0:T(8,128)(2,1)S(1)}, u32[]{:S(2)}, u32[]{:S(2)}) collective-permute-start(bf16[64,512]{1,0:T(8,128)(2,1)} %bitcast.22), channel_id=1, source_target_pairs={{0,0},{2,128},{4,256},{6,384},{128,2},{130,130},{132,258},{134,386... | collective-permute-start | bytes 196616 | tf_op jit(solution)/shard_map/ppermute | solution.py:103
  8.0 5.6 %collective-permute-start.1 = (bf16[64,512]{1,0:T(8,128)(2,1)}, bf16[64,512]{1,0:T(8,128)(2,1)S(1)}, u32[]{:S(2)}, u32[]{:S(2)}) collective-permute-start(bf16[64,512]{1,0:T(8,128)(2,1)} %bitcast.23), channel_id=1, source_target_pairs={{0,128},{2,256},{4,384},{6,0},{128,130},{130,258},{132,386},{134,2... | collective-permute-start | bytes 196616 | tf_op jit(solution)/shard_map/ppermute | solution.py:103
  13.7 6.2 %collective-permute-start.2 = (bf16[64,512]{1,0:T(8,128)(2,1)}, bf16[64,512]{1,0:T(8,128)(2,1)S(1)}, u32[]{:S(2)}, u32[]{:S(2)}) collective-permute-start(bf16[64,512]{1,0:T(8,128)(2,1)} %bitcast.24), channel_id=1, source_target_pairs={{0,256},{2,384},{4,0},{6,128},{128,258},{130,386},{132,2},{134,130... | collective-permute-start | bytes 196616 | tf_op jit(solution)/shard_map/ppermute | solution.py:103
  19.8 3.8 %collective-permute-start.3 = (bf16[64,512]{1,0:T(8,128)(2,1)}, bf16[64,512]{1,0:T(8,128)(2,1)S(1)}, u32[]{:S(2)}, u32[]{:S(2)}) collective-permute-start(bf16[64,512]{1,0:T(8,128)(2,1)} %bitcast.25), channel_id=1, source_target_pairs={{0,384},{2,0},{4,128},{6,256},{128,386},{130,2},{132,130},{134,258... | collective-permute-start | bytes 196616 | tf_op jit(solution)/shard_map/ppermute | solution.py:103
  23.6 0.0 copy-start.1
  23.6 1.0 copy-done.1
  24.6 0.0 copy-start.3
  24.6 1.0 copy-done.3
  25.7 0.0 copy-start.2
  25.7 0.0 copy-start.4
  25.7 1.2 shard_map.46
  26.9 0.0 collective-permute-done
  26.9 0.0 collective-permute-done.1
  26.9 0.0 collective-permute-done.2
  26.9 0.0 collective-permute-done.3
  26.9 0.7 pad_maximum_fusion
  27.6 0.0 all-gather.3.cloned.1.call-update
  27.7 32.2 %all_to_all.15.s_ref = bf16[64,8,128]{2,1,0:T(8,128)(2,1)S(1)} all-to-all(bf16[64,8,128]{2,1,0:T(8,128)(2,1)S(1)} %bitcast.14), channel_id=1, replica_groups=mesh['x'=4,'z'=16,'y'=4,'c'=2] {'x','z'}, dimensions={0} | all-to-all | bytes 262144 | tf_op jit(solution)/shard_map/all_to_all | solution.py:120
  59.9 0.1 shard_map.47
  59.9 19.7 %all_to_all.16 = bf16[64,8,128]{2,1,0:T(8,128)(2,1)S(1)} all-to-all(bf16[64,8,128]{2,1,0:T(8,128)(2,1)S(1)} %shard_map.47), channel_id=1, replica_groups=mesh['x'=4,'z'=16,'y'=4,'c'=2] {'x','z'}, dimensions={0} | all-to-all | bytes 262144 | tf_op jit(solution)/shard_map/all_to_all | solution.py:124
  79.7 0.0 copy-done.2
  79.7 0.0 copy-done.4
  79.7 0.0 copy-start.5
  79.7 1.0 copy-done.5
  80.7 3.5 %shard_map.48 = bf16[4,512,512]{2,1,0:T(8,128)(2,1)S(1)} custom-call(bf16[512,512]{1,0:T(8,128)(2,1)S(1)} %copy-done.5, bf16[512,512]{1,0:T(8,128)(2,1)S(1)} %copy-done.2, bf16[512,512]{1,0:T(8,128)(2,1)S(1)} %copy-done.4, bf16[512,128]{1,0:T(8,128)(2,1)S(1)} %bitcast.15), custom_call_target="tpu_custom_call" | custom-call | tf_op jit(solution)/shard_map/pallas_call | solution.py:125
  84.2 0.0 copy-start
  84.2 1.3 copy-done
  85.6 3.6 %all-to-all-start.2 = ((bf16[4,512,512]{2,1,0:T(8,128)(2,1)}), bf16[4,512,512]{2,1,0:T(8,128)(2,1)S(1)}, u32[]{:S(2)}, u32[]{:S(2)}) async-start(bf16[4,512,512]{2,1,0:T(8,128)(2,1)} %copy-done), calls=%async_computation.2 | async-start | bytes 4194304 | tf_op jit(solution)/shard_map/all_to_all | solution.py:133
  89.3 0.1 stack.55.order_ref
  89.3 19.8 %all-to-all-done.2.h_ref = bf16[4,512,512]{2,1,0:T(8,128)(2,1)S(1)} async-done(((bf16[4,512,512]{2,1,0:T(8,128)(2,1)}), bf16[4,512,512]{2,1,0:T(8,128)(2,1)S(1)}, u32[]{:S(2)}, u32[]{:S(2)}) %all-to-all-start.2) | async-done | bytes 2097184 | tf_op jit(solution)/shard_map/all_to_all | solution.py:133
  109.1 1.5 %all-gather.3.cloned.1.call-done = bf16[64,64,512]{2,1,0:T(8,128)(2,1)} async-done(((bf16[4,64,512]{2,1,0:T(8,128)(2,1)}), bf16[64,64,512]{2,1,0:T(8,128)(2,1)}) %all-gather.3.cloned.1.call-update) | async-done | bytes 4194320 | tf_op jit(solution)/shard_map/all_gather | solution.py:118
  110.6 3.3 %shard_map.50 = bf16[512,512]{1,0:T(8,128)(2,1)S(1)} custom-call(s32[5]{0:T(128)S(1)} %stack.55.order_ref, bf16[4,512,512]{2,1,0:T(8,128)(2,1)S(1)} %all-to-all-done.2.h_ref, bf16[16,4,64,512]{3,2,1,0:T(8,128)(2,1)} %bitcast.16), custom_call_target="tpu_custom_call" | custom-call | tf_op jit(solution)/shard_map/pallas_call | solution.py:77
  113.9 9.4 %collective-permute-start.4 = (bf16[512,512]{1,0:T(8,128)(2,1)S(1)}, bf16[512,512]{1,0:T(8,128)(2,1)S(1)}, u32[]{:S(2)}, u32[]{:S(2)}) collective-permute-start(bf16[512,512]{1,0:T(8,128)(2,1)S(1)} %shard_map.50), channel_id=1, source_target_pairs={{0,1},{1,0},{2,3},{3,2},{4,5},{5,4},{6,7},{7,6},{8,9},{9,8},{10,11... | collective-permute-start | bytes 1572872 | tf_op jit(solution)/shard_map/ppermute | solution.py:138
  123.4 0.1 stack.48.order_ref
  123.5 3.3 %shard_map.49.a_ref = f32[512,512]{1,0:T(8,128)S(1)} custom-call(s32[5]{0:T(128)S(1)} %stack.48.order_ref, bf16[4,512,512]{2,1,0:T(8,128)(2,1)S(1)} %all-to-all-done.2.h_ref, bf16[16,4,64,512]{3,2,1,0:T(8,128)(2,1)} %bitcast.17), custom_call_target="tpu_custom_call" | custom-call | tf_op jit(solution)/shard_map/pallas_call | solution.py:77
  126.8 0.0 collective-permute-done.4.b_ref
  126.8 0.9 shard_map.51
Async XLA Ops:
  6.5 104.1 %all-gather.3.cloned.1.call-start = ((), (), s32[]{:S(2)}) async-start(), calls=%async_computation.3 | async-start | bytes 4456448 | tf_op jit(solution)/shard_map/all_gather | solution.py:118
  6.5 20.3 %collective-permute-start = (bf16[64,512]{1,0:T(8,128)(2,1)}, bf16[64,512]{1,0:T(8,128)(2,1)S(1)}, u32[]{:S(2)}, u32[]{:S(2)}) collective-permute-start(bf16[64,512]{1,0:T(8,128)(2,1)} %bitcast.22), channel_id=1, source_target_pairs={{0,0},{2,128},{4,256},{6,384},{128,2},{130,130},{132,258},{134,386... | collective-permute-start | bytes 196616 | tf_op jit(solution)/shard_map/ppermute | solution.py:103
  8.0 18.9 %collective-permute-start.1 = (bf16[64,512]{1,0:T(8,128)(2,1)}, bf16[64,512]{1,0:T(8,128)(2,1)S(1)}, u32[]{:S(2)}, u32[]{:S(2)}) collective-permute-start(bf16[64,512]{1,0:T(8,128)(2,1)} %bitcast.23), channel_id=1, source_target_pairs={{0,128},{2,256},{4,384},{6,0},{128,130},{130,258},{132,386},{134,2... | collective-permute-start | bytes 196616 | tf_op jit(solution)/shard_map/ppermute | solution.py:103
  13.7 13.2 %collective-permute-start.2 = (bf16[64,512]{1,0:T(8,128)(2,1)}, bf16[64,512]{1,0:T(8,128)(2,1)S(1)}, u32[]{:S(2)}, u32[]{:S(2)}) collective-permute-start(bf16[64,512]{1,0:T(8,128)(2,1)} %bitcast.24), channel_id=1, source_target_pairs={{0,256},{2,384},{4,0},{6,128},{128,258},{130,386},{132,2},{134,130... | collective-permute-start | bytes 196616 | tf_op jit(solution)/shard_map/ppermute | solution.py:103
  19.8 7.1 %collective-permute-start.3 = (bf16[64,512]{1,0:T(8,128)(2,1)}, bf16[64,512]{1,0:T(8,128)(2,1)S(1)}, u32[]{:S(2)}, u32[]{:S(2)}) collective-permute-start(bf16[64,512]{1,0:T(8,128)(2,1)} %bitcast.25), channel_id=1, source_target_pairs={{0,384},{2,0},{4,128},{6,256},{128,386},{130,2},{132,130},{134,258... | collective-permute-start | bytes 196616 | tf_op jit(solution)/shard_map/ppermute | solution.py:103
  23.6 1.0 copy-start.1
  24.6 1.0 copy-start.3
  25.7 54.0 %copy-start.2 = (bf16[512,512]{1,0:T(8,128)(2,1)S(1)}, bf16[512,512]{1,0:T(8,128)(2,1)}, u32[]{:S(2)}) copy-start(bf16[512,512]{1,0:T(8,128)(2,1)} %k_ref.3) | copy-start | bytes 1572868
  25.7 54.0 %copy-start.4 = (bf16[512,512]{1,0:T(8,128)(2,1)S(1)}, bf16[512,512]{1,0:T(8,128)(2,1)}, u32[]{:S(2)}) copy-start(bf16[512,512]{1,0:T(8,128)(2,1)} %v_ref.3) | copy-start | bytes 1572868
  79.7 1.0 copy-start.5
  84.2 1.3 copy-start
  85.6 23.5 %all-to-all-start.2 = ((bf16[4,512,512]{2,1,0:T(8,128)(2,1)}), bf16[4,512,512]{2,1,0:T(8,128)(2,1)S(1)}, u32[]{:S(2)}, u32[]{:S(2)}) async-start(bf16[4,512,512]{2,1,0:T(8,128)(2,1)} %copy-done), calls=%async_computation.2 | async-start | bytes 4194304 | tf_op jit(solution)/shard_map/all_to_all | solution.py:133
  113.9 12.9 %collective-permute-start.4 = (bf16[512,512]{1,0:T(8,128)(2,1)S(1)}, bf16[512,512]{1,0:T(8,128)(2,1)S(1)}, u32[]{:S(2)}, u32[]{:S(2)}) collective-permute-start(bf16[512,512]{1,0:T(8,128)(2,1)S(1)} %shard_map.50), channel_id=1, source_target_pairs={{0,1},{1,0},{2,3},{3,2},{4,5},{5,4},{6,7},{7,6},{8,9},{9,8},{10,11... | collective-permute-start | bytes 1572872 | tf_op jit(solution)/shard_map/ppermute | solution.py:138
Sparse Core Ops, SparseCore 0:
  27.8 82.7 all-gather.2

commit v3 on v2

--- a/solution.py
+++ b/solution.py
@@ -55,10 +55,10 @@
 
 
 def projection_kernel(order_ref, h_ref, w_ref, o_ref):
-    blocks, _, cols, depth = w_ref.shape
+    blocks, sources, cols, depth = w_ref.shape
     total = None
-    for y in range(h_ref.shape[0]):
-        w = w_ref[:, order_ref[1 + y]].reshape(blocks * cols, depth)
+    for y in range(sources):
+        w = w_ref[:, y].reshape(blocks * cols, depth)
         part = lax.dot_general(h_ref[y], w, (((1,), (1,)), ((), ())), preferred_element_type=F32)
         total = part if total is None else total + part
     o_ref[...] = total.astype(o_ref.dtype)
@@ -70,7 +70,7 @@
 
 def project(order, hidden, w_all, dtype):
     sources, rows, depth = hidden.shape
-    slots, cols = w_all.shape[1:3]
+    cols = w_all.shape[2]
     zb = 4
     width = NZ // NC * cols
     steps = NZ // NC // zb
@@ -80,12 +80,15 @@
             num_scalar_prefetch=1,
             grid=(steps,),
             in_specs=[
-                pl.BlockSpec((sources, rows, depth), lambda n, order: (0, 0, 0)),
-                pl.BlockSpec((zb, slots, cols, depth), lambda n, order: (order[0] * steps + n, 0, 0, 0)),
+                pl.BlockSpec(memory_space=pltpu.VMEM),
+                pl.BlockSpec((zb, sources, cols, depth), lambda n, order: (order[0] * steps + n, 0, 0, 0)),
             ],
             out_specs=pl.BlockSpec((rows, zb * cols), lambda n, order: (0, n)),
         ),
         out_shape=jax.ShapeDtypeStruct((rows, width), dtype),
+        cost_estimate=pl.CostEstimate(
+            flops=2 * rows * width * sources * depth, bytes_accessed=4 << 20, transcendentals=0
+        ),
         compiler_params=params(),
     )(order, hidden, w_all)
 
@@ -96,16 +99,12 @@
 def local(queries, keys, values, out_weight):
     rows, width = queries.shape
     heads = width // HEAD_DIM
-    me_x, me_c = lax.axis_index("x"), lax.axis_index("c")
+    me_c = lax.axis_index("c")
 
-    w = out_weight.T
-    w4 = jnp.stack([
-        lax.ppermute(
-            w, ("x", "y"),
-            [(x * NY + y, (y + k) % NX * NY + x) for x in range(NX) for y in range(NY)],
-        )
-        for k in range(NX)
-    ])
+    w = lax.ppermute(
+        out_weight.T, ("x", "y"),
+        [(x * NY + y, y * NY + x) for x in range(NX) for y in range(NY)],
+    )
     by_head = pl.BlockSpec((rows, HEAD_DIM), lambda h: (0, h))
     state = pl.BlockSpec((HEAD_DIM, HEAD_DIM), lambda h: (h, 0))
     states = pl.pallas_call(
@@ -114,6 +113,8 @@
         out_shape=jax.ShapeDtypeStruct((width, HEAD_DIM), BF),
         in_specs=[by_head, by_head], out_specs=state, compiler_params=params(),
     )(keys, values)
+    states, w = lax.optimization_barrier((states, w))
+    w4 = lax.all_to_all(jnp.broadcast_to(w[None], (NX,) + w.shape), "x", 0, 0)
     states, w4 = lax.optimization_barrier((states, w4))
     w_all = lax.all_gather(w4, "z")
     part = width // N_CTX
@@ -131,9 +132,8 @@
         compiler_params=params(),
     )(queries, keys, values, prefix)
     hidden = lax.all_to_all(hidden, "y", 0, 0)
-    slots = [(me_x - y) % NX for y in range(NY)]
-    away = jnp.stack([1 - me_c] + slots).astype(jnp.int32)
-    home = jnp.stack([me_c] + slots).astype(jnp.int32)
+    away = (1 - me_c).astype(jnp.int32).reshape(1)
+    home = me_c.astype(jnp.int32).reshape(1)
     other = project(away, hidden, w_all, BF)
     other = lax.ppermute(other, "c", [(0, 1), (1, 0)])
     own = project(home, hidden, w_all, F32)

time: 135 us -> 131 us (0.970)
  starting transfers between devices: 30.1 us -> 15.2 us
  blocking collectives: 51.9 us -> 65.2 us
    ppermute x4 -> x1, starting transfers between devices: 17 us -> 1.49 us  [local(): lax.ppermute(out_weight.T, ('x', 'y'), [(x * NY + y, y * NY + x) for x in...]
    all_to_all x0 -> x1, blocking collectives: none -> 14.9 us  [local(): w4 = lax.all_to_all(jnp.broadcast_to(w[None], (NX,) + w.shape), 'x', 0, 0)]
    all_to_all x1, blocking collectives: 32.2 us -> 30.2 us  [local(): lax.all_to_all(states.reshape(N_CTX, part, HEAD_DIM), ('x', 'z'), 0, 0)]
    all_gather x1, waiting for transfers between devices: 1.49 us -> 2.87 us  [local(): w_all = lax.all_gather(w4, 'z')]
  transfers between devices with their start and end apart: 7 -> 4, of which waited for: 2 -> 2; matrix products, arithmetic and copies ran while one was open for 0% -> 0% of each run, Pallas kernels for 6% -> 6%
where the time goes in v3:
time: 131 us
  blocking collectives  65.2 us (50%)
  waiting for transfers between devices  22.4 us (17%)
  starting transfers between devices  15.2 us (12%)
  between operations  13.5 us (10%)
  Pallas kernels  11.2 us (9%)
  local copies, waits for them, and re-layouts  3.42 us (3%)
    all_to_all x1, blocking collectives, local(): lax.all_to_all(states.reshape(N_CTX, part, HEAD_DIM), ('x', 'z'), 0, 0)  30.2 us
    all_to_all x1, blocking collectives, local(): prefix = lax.all_to_all(scanned, ('x', 'z'), 0, 0).reshape(width, HEAD_DIM)  20.1 us
    all_to_all x1, waiting for transfers between devices, local(): hidden = lax.all_to_all(hidden, 'y', 0, 0)  19.5 us
    all_to_all x1, blocking collectives, local(): w4 = lax.all_to_all(jnp.broadcast_to(w[None], (NX,) + w.shape), 'x', 0, 0)  14.9 us
    ppermute x1, starting transfers between devices, local(): other = lax.ppermute(other, 'c', [(0, 1), (1, 0)])  10.1 us
    pallas_call x2, Pallas kernels, project(): pl.pallas_call(projection_kernel, grid_spec=pltpu.PrefetchScalarGridSpec(...  5.55 us
    all_to_all x1, starting transfers between devices, local(): hidden = lax.all_to_all(hidden, 'y', 0, 0)  3.62 us
    pallas_call x1, Pallas kernels, local(): pl.pallas_call(attention_kernel, grid=(heads,), out_shape=jax.ShapeDtypeS...  3.52 us
  transfers between devices with their start and end apart: 4, of which 2 were waited for; matrix products, arithmetic and copies ran while one was open for 0% of the time, Pallas kernels for 6%

profile of v3, /device:TPU:1, one launch (start us, length us, event | category | flops | bytes accessed | tf_op | source)
XLA Modules:
  0.0 130.9 jit_solution(16881037711487598105)
XLA Ops:
  6.5 0.0 all-gather.3.cloned.1.call-start
  6.5 1.5 %collective-permute-start = (bf16[64,512]{1,0:T(8,128)(2,1)}, bf16[64,512]{1,0:T(8,128)(2,1)S(1)}, u32[]{:S(2)}, u32[]{:S(2)}) collective-permute-start(bf16[64,512]{1,0:T(8,128)(2,1)} %bitcast.10), channel_id=1, source_target_pairs={{0,0},{2,128},{4,256},{6,384},{128,2},{130,130},{132,258},{134,386... | collective-permute-start | bytes 196616 | tf_op jit(solution)/shard_map/ppermute | solution.py:104
  8.0 0.0 copy-start.1
  8.0 1.0 copy-done.1
  9.1 0.0 copy-start.3
  9.1 1.0 copy-done.3
  10.1 0.0 copy-start.2
  10.1 0.0 copy-start.4
  10.1 0.0 copy-start.5
  10.1 1.2 shard_map.46
  11.3 0.0 collective-permute-done
  11.3 14.9 %all_to_all.20 = bf16[4,64,512]{2,1,0:T(8,128)(2,1)} all-to-all(bf16[4,64,512]{2,1,0:T(8,128)(2,1)S(1)} %broadcast_in_dim.2), channel_id=1, replica_groups=mesh['x'=4,'z'=16,'y'=4,'c'=2] {'x'}, dimensions={0} | all-to-all | bytes 524288 | tf_op jit(solution)/shard_map/all_to_all | solution.py:117
  26.3 0.0 all-gather.3.cloned.1.call-update
  26.3 30.2 %all_to_all.21.s_ref = bf16[64,8,128]{2,1,0:T(8,128)(2,1)S(1)} all-to-all(bf16[64,8,128]{2,1,0:T(8,128)(2,1)S(1)} %bitcast.6), channel_id=1, replica_groups=mesh['x'=4,'z'=16,'y'=4,'c'=2] {'x','z'}, dimensions={0} | all-to-all | bytes 262144 | tf_op jit(solution)/shard_map/all_to_all | solution.py:121
  56.5 0.1 shard_map.47
  56.6 20.1 %all_to_all.22 = bf16[64,8,128]{2,1,0:T(8,128)(2,1)S(1)} all-to-all(bf16[64,8,128]{2,1,0:T(8,128)(2,1)S(1)} %shard_map.47), channel_id=1, replica_groups=mesh['x'=4,'z'=16,'y'=4,'c'=2] {'x','z'}, dimensions={0} | all-to-all | bytes 262144 | tf_op jit(solution)/shard_map/all_to_all | solution.py:125
  76.7 0.0 copy-done.2
  76.7 0.0 copy-done.4
  76.7 0.0 copy-done.5
  76.7 3.5 %shard_map.48 = bf16[4,512,512]{2,1,0:T(8,128)(2,1)S(1)} custom-call(bf16[512,512]{1,0:T(8,128)(2,1)S(1)} %copy-done.5, bf16[512,512]{1,0:T(8,128)(2,1)S(1)} %copy-done.2, bf16[512,512]{1,0:T(8,128)(2,1)S(1)} %copy-done.4, bf16[512,128]{1,0:T(8,128)(2,1)S(1)} %bitcast.7), custom_call_target="tpu_custom_call" | custom-call | tf_op jit(solution)/shard_map/pallas_call | solution.py:126
  80.2 0.0 copy-start
  80.2 1.3 %copy-done = bf16[4,512,512]{2,1,0:T(8,128)(2,1)} copy-done((bf16[4,512,512]{2,1,0:T(8,128)(2,1)}, bf16[4,512,512]{2,1,0:T(8,128)(2,1)S(1)}, u32[]{:S(2)}) %copy-start) | copy-done | bytes 2097176
  81.5 3.6 %all-to-all-start.3 = ((bf16[4,512,512]{2,1,0:T(8,128)(2,1)}), bf16[4,512,512]{2,1,0:T(8,128)(2,1)S(1)}, u32[]{:S(2)}, u32[]{:S(2)}) async-start(bf16[4,512,512]{2,1,0:T(8,128)(2,1)} %copy-done), calls=%async_computation.3 | async-start | bytes 4194304 | tf_op jit(solution)/shard_map/all_to_all | solution.py:134
  85.1 19.5 %all-to-all-done.3.h_ref = bf16[4,512,512]{2,1,0:T(8,128)(2,1)S(1)} async-done(((bf16[4,512,512]{2,1,0:T(8,128)(2,1)}), bf16[4,512,512]{2,1,0:T(8,128)(2,1)S(1)}, u32[]{:S(2)}, u32[]{:S(2)}) %all-to-all-start.3) | async-done | bytes 2097184 | tf_op jit(solution)/shard_map/all_to_all | solution.py:134
  104.6 2.9 %all-gather.3.cloned.1.call-done = bf16[64,64,512]{2,1,0:T(8,128)(2,1)} async-done(((bf16[4,64,512]{2,1,0:T(8,128)(2,1)}), bf16[64,64,512]{2,1,0:T(8,128)(2,1)}) %all-gather.3.cloned.1.call-update) | async-done | bytes 4194320 | tf_op jit(solution)/shard_map/all_gather | solution.py:119
  107.5 2.7 %shard_map.50 = bf16[512,512]{1,0:T(8,128)(2,1)S(1)} custom-call(s32[1]{0:T(128)} %bitcast.5.order_ref, bf16[4,512,512]{2,1,0:T(8,128)(2,1)S(1)} %all-to-all-done.3.h_ref, bf16[16,4,64,512]{3,2,1,0:T(8,128)(2,1)} %bitcast.8), custom_call_target="tpu_custom_call" | custom-call | flops 1073741824 | bytes 4194304 | tf_op jit(solution)/shard_map/pallas_call | solution.py:77
  110.3 10.1 %collective-permute-start.1 = (bf16[512,512]{1,0:T(8,128)(2,1)S(1)}, bf16[512,512]{1,0:T(8,128)(2,1)S(1)}, u32[]{:S(2)}, u32[]{:S(2)}) collective-permute-start(bf16[512,512]{1,0:T(8,128)(2,1)S(1)} %shard_map.50), channel_id=1, source_target_pairs={{0,1},{1,0},{2,3},{3,2},{4,5},{5,4},{6,7},{7,6},{8,9},{9,8},{10,11... | collective-permute-start | bytes 1572872 | tf_op jit(solution)/shard_map/ppermute | solution.py:138
  120.4 2.8 %shard_map.49.a_ref = f32[512,512]{1,0:T(8,128)S(1)} custom-call(s32[1]{0:T(128)} %bitcast.order_ref, bf16[4,512,512]{2,1,0:T(8,128)(2,1)S(1)} %all-to-all-done.3.h_ref, bf16[16,4,64,512]{3,2,1,0:T(8,128)(2,1)} %bitcast.9), custom_call_target="tpu_custom_call" | custom-call | flops 1073741824 | bytes 4194304 | tf_op jit(solution)/shard_map/pallas_call | solution.py:77
  123.2 0.0 collective-permute-done.1.b_ref
  123.2 0.9 shard_map.51
  (1 shorter events, 0.0 us)
Async XLA Ops:
  6.5 101.0 %all-gather.3.cloned.1.call-start = ((), (), s32[]{:S(2)}) async-start(), calls=%async_computation.4 | async-start | bytes 4456448 | tf_op jit(solution)/shard_map/all_gather | solution.py:119
  6.5 4.8 %collective-permute-start = (bf16[64,512]{1,0:T(8,128)(2,1)}, bf16[64,512]{1,0:T(8,128)(2,1)S(1)}, u32[]{:S(2)}, u32[]{:S(2)}) collective-permute-start(bf16[64,512]{1,0:T(8,128)(2,1)} %bitcast.10), channel_id=1, source_target_pairs={{0,0},{2,128},{4,256},{6,384},{128,2},{130,130},{132,258},{134,386... | collective-permute-start | bytes 196616 | tf_op jit(solution)/shard_map/ppermute | solution.py:104
  8.0 1.0 copy-start.1
  9.1 1.0 copy-start.3
  10.1 66.5 %copy-start.2 = (bf16[512,512]{1,0:T(8,128)(2,1)S(1)}, bf16[512,512]{1,0:T(8,128)(2,1)}, u32[]{:S(2)}) copy-start(bf16[512,512]{1,0:T(8,128)(2,1)} %k_ref.3) | copy-start | bytes 1572868
  10.1 66.5 %copy-start.4 = (bf16[512,512]{1,0:T(8,128)(2,1)S(1)}, bf16[512,512]{1,0:T(8,128)(2,1)}, u32[]{:S(2)}) copy-start(bf16[512,512]{1,0:T(8,128)(2,1)} %v_ref.3) | copy-start | bytes 1572868
  10.1 66.6 %copy-start.5 = (bf16[512,512]{1,0:T(8,128)(2,1)S(1)}, bf16[512,512]{1,0:T(8,128)(2,1)}, u32[]{:S(2)}) copy-start(bf16[512,512]{1,0:T(8,128)(2,1)} %q_ref.1) | copy-start | bytes 1572868
  80.2 1.3 %copy-start = (bf16[4,512,512]{2,1,0:T(8,128)(2,1)}, bf16[4,512,512]{2,1,0:T(8,128)(2,1)S(1)}, u32[]{:S(2)}) copy-start(bf16[4,512,512]{2,1,0:T(8,128)(2,1)S(1)} %shard_map.48) | copy-start | bytes 6291460
  81.5 23.1 %all-to-all-start.3 = ((bf16[4,512,512]{2,1,0:T(8,128)(2,1)}), bf16[4,512,512]{2,1,0:T(8,128)(2,1)S(1)}, u32[]{:S(2)}, u32[]{:S(2)}) async-start(bf16[4,512,512]{2,1,0:T(8,128)(2,1)} %copy-done), calls=%async_computation.3 | async-start | bytes 4194304 | tf_op jit(solution)/shard_map/all_to_all | solution.py:134
  110.3 12.9 %collective-permute-start.1 = (bf16[512,512]{1,0:T(8,128)(2,1)S(1)}, bf16[512,512]{1,0:T(8,128)(2,1)S(1)}, u32[]{:S(2)}, u32[]{:S(2)}) collective-permute-start(bf16[512,512]{1,0:T(8,128)(2,1)S(1)} %shard_map.50), channel_id=1, source_target_pairs={{0,1},{1,0},{2,3},{3,2},{4,5},{5,4},{6,7},{7,6},{8,9},{9,8},{10,11... | collective-permute-start | bytes 1572872 | tf_op jit(solution)/shard_map/ppermute | solution.py:138
Sparse Core Ops, SparseCore 0:
  26.4 81.0 all-gather.2

commit v4 on v3

--- a/solution.py
+++ b/solution.py
@@ -54,43 +54,48 @@
             o_ref[n, here, :] = hidden
 
 
-def projection_kernel(order_ref, h_ref, w_ref, o_ref):
-    blocks, sources, cols, depth = w_ref.shape
-    total = None
-    for y in range(sources):
-        w = w_ref[:, y].reshape(blocks * cols, depth)
-        part = lax.dot_general(h_ref[y], w, (((1,), (1,)), ((), ())), preferred_element_type=F32)
-        total = part if total is None else total + part
-    o_ref[...] = total.astype(o_ref.dtype)
+def projection_kernel(core_ref, own_ref, other_ref, w_ref, o_ref, acc_ref):
+    blocks, _, sources, cols, depth = w_ref.shape
+
+    def part(h_ref):
+        total = None
+        for y in range(sources):
+            w = w_ref[:, 0, y].reshape(blocks * cols, depth)
+            one = lax.dot_general(h_ref[y], w, (((1,), (1,)), ((), ())), preferred_element_type=F32)
+            total = one if total is None else total + one
+        return total
+
+    @pl.when(pl.program_id(1) == 0)
+    def _():
+        acc_ref[...] = part(own_ref)
+
+    @pl.when(pl.program_id(1) == 1)
+    def _():
+        o_ref[...] = (acc_ref[...] + part(other_ref)).astype(o_ref.dtype)
 
 
-def add_kernel(a_ref, b_ref, o_ref):
-    o_ref[...] = (a_ref[...] + b_ref[...].astype(F32)).astype(BF)
-
-
-def project(order, hidden, w_all, dtype):
-    sources, rows, depth = hidden.shape
-    cols = w_all.shape[2]
+def project(core, own, other, w_all):
+    sources, rows, depth = own.shape
+    cols = w_all.shape[3]
     zb = 4
-    width = NZ // NC * cols
     steps = NZ // NC // zb
     return pl.pallas_call(
         projection_kernel,
         grid_spec=pltpu.PrefetchScalarGridSpec(
             num_scalar_prefetch=1,
-            grid=(steps,),
-            in_specs=[
-                pl.BlockSpec(memory_space=pltpu.VMEM),
-                pl.BlockSpec((zb, sources, cols, depth), lambda n, order: (order[0] * steps + n, 0, 0, 0)),
+            grid=(steps, NC),
+            in_specs=[pl.BlockSpec(memory_space=pltpu.VMEM)] * 2 + [
+                pl.BlockSpec(
+                    (zb, 1, sources, cols, depth),
+                    lambda n, k, core: (core[0] * steps + n, core[0] ^ k, 0, 0, 0),
+                ),
             ],
-            out_specs=pl.BlockSpec((rows, zb * cols), lambda n, order: (0, n)),
+            out_specs=pl.BlockSpec((rows, zb * cols), lambda n, k, core: (0, n)),
+            scratch_shapes=[pltpu.VMEM((rows, zb * cols), F32)],
         ),
-        out_shape=jax.ShapeDtypeStruct((rows, width), dtype),
-        cost_estimate=pl.CostEstimate(
-            flops=2 * rows * width * sources * depth, bytes_accessed=4 << 20, transcendentals=0
-        ),
+        out_shape=jax.ShapeDtypeStruct((rows, NZ // NC * cols), BF),
         compiler_params=params(),
-    )(order, hidden, w_all)
+    )(core, own, other, w_all)
 
 
 AXES = ("x", "z", "y", "c")
@@ -116,7 +121,7 @@
     states, w = lax.optimization_barrier((states, w))
     w4 = lax.all_to_all(jnp.broadcast_to(w[None], (NX,) + w.shape), "x", 0, 0)
     states, w4 = lax.optimization_barrier((states, w4))
-    w_all = lax.all_gather(w4, "z")
+    w_all = lax.all_gather(w4, ("z", "c")).reshape((NZ, NC) + w4.shape)
     part = width // N_CTX
     mine = lax.all_to_all(states.reshape(N_CTX, part, HEAD_DIM), ("x", "z"), 0, 0)
     scanned = pl.pallas_call(
@@ -132,18 +137,8 @@
         compiler_params=params(),
     )(queries, keys, values, prefix)
     hidden = lax.all_to_all(hidden, "y", 0, 0)
-    away = (1 - me_c).astype(jnp.int32).reshape(1)
-    home = me_c.astype(jnp.int32).reshape(1)
-    other = project(away, hidden, w_all, BF)
-    other = lax.ppermute(other, "c", [(0, 1), (1, 0)])
-    own = project(home, hidden, w_all, F32)
-    tile = pl.BlockSpec((rows // 2, width), lambda n: (n, 0))
-    return pl.pallas_call(
-        add_kernel,
-        grid=(2,),
-        out_shape=jax.ShapeDtypeStruct((rows, width), BF),
-        in_specs=[tile, tile], out_specs=tile, compiler_params=params(),
-    )(own, other)
+    other = lax.ppermute(hidden, "c", [(0, 1), (1, 0)])
+    return project(me_c.astype(jnp.int32).reshape(1), hidden, other, w_all)
 
 
 def solution(mesh):

time: 131 us -> 130 us (level)
  blocking collectives: 65.2 us -> 88.1 us
  waiting for transfers between devices: 22.4 us -> 4.33 us
  starting transfers between devices: 15.2 us -> 10.9 us
  local copies, waits for them, and re-layouts: 3.42 us -> 2.11 us
    all_to_all x0 -> x1, blocking collectives: none -> 22.8 us  [local(): hidden = lax.all_to_all(hidden, 'y', 0, 0)]
    all_to_all x1 -> x0, waiting for transfers between devices: 19.5 us -> none  [local(): hidden = lax.all_to_all(hidden, 'y', 0, 0)]
    ppermute x1, waiting for transfers between devices: 0.01 us -> 3.89 us  [local(): other = lax.ppermute(hidden, 'c', [(0, 1), (1, 0)])]
    all_to_all x1 -> x0, starting transfers between devices: 3.62 us -> none  [local(): hidden = lax.all_to_all(hidden, 'y', 0, 0)]
    all_gather x1, waiting for transfers between devices: 2.87 us -> 0.41 us  [local(): w_all = lax.all_gather(w4, ('z', 'c')).reshape((NZ, NC) + w4.shape)]
    unnamed x12 -> x10, local copies, waits for them, and re-layouts: 3.41 us -> 2.09 us
    pallas_call x2 -> x1, Pallas kernels: 5.55 us -> 6.33 us  [project(): pl.pallas_call(projection_kernel, grid_spec=pltpu.PrefetchScalarGridSpec(...]
  transfers between devices with their start and end apart: 4 -> 3, of which waited for: 2 -> 2; matrix products, arithmetic and copies ran while one was open for 0% -> 0% of each run, Pallas kernels for 6% -> 4%
where the time goes in v4:
time: 130 us
  blocking collectives  88.1 us (68%)
  between operations  13.4 us (10%)
  Pallas kernels  11.1 us (9%)
  starting transfers between devices  10.9 us (8%)
  waiting for transfers between devices  4.33 us (3%)
  local copies, waits for them, and re-layouts  2.11 us (2%)
    all_to_all x1, blocking collectives, local(): lax.all_to_all(states.reshape(N_CTX, part, HEAD_DIM), ('x', 'z'), 0, 0)  30.2 us
    all_to_all x1, blocking collectives, local(): hidden = lax.all_to_all(hidden, 'y', 0, 0)  22.8 us
    all_to_all x1, blocking collectives, local(): prefix = lax.all_to_all(scanned, ('x', 'z'), 0, 0).reshape(width, HEAD_DIM)  20.1 us
    all_to_all x1, blocking collectives, local(): w4 = lax.all_to_all(jnp.broadcast_to(w[None], (NX,) + w.shape), 'x', 0, 0)  14.9 us
    ppermute x1, starting transfers between devices, local(): other = lax.ppermute(hidden, 'c', [(0, 1), (1, 0)])  9.38 us
    pallas_call x1, Pallas kernels, project(): pl.pallas_call(projection_kernel, grid_spec=pltpu.PrefetchScalarGridSpec(...  6.33 us
    ppermute x1, waiting for transfers between devices, local(): other = lax.ppermute(hidden, 'c', [(0, 1), (1, 0)])  3.89 us
    pallas_call x1, Pallas kernels, local(): pl.pallas_call(attention_kernel, grid=(heads,), out_shape=jax.ShapeDtypeS...  3.52 us
  transfers between devices with their start and end apart: 3, of which 2 were waited for; matrix products, arithmetic and copies ran while one was open for 0% of the time, Pallas kernels for 4%

profile of v4, /device:TPU:1, one launch (start us, length us, event | category | flops | bytes accessed | tf_op | source)
XLA Modules:
  0.0 129.9 jit_solution(4537429322126974816)
XLA Ops:
  6.5 0.0 all-gather.3.cloned.1.call-start
  6.5 1.5 %collective-permute-start = (bf16[64,512]{1,0:T(8,128)(2,1)}, bf16[64,512]{1,0:T(8,128)(2,1)S(1)}, u32[]{:S(2)}, u32[]{:S(2)}) collective-permute-start(bf16[64,512]{1,0:T(8,128)(2,1)} %bitcast.8), channel_id=1, source_target_pairs={{0,0},{2,128},{4,256},{6,384},{128,2},{130,130},{132,258},{134,386... | collective-permute-start | bytes 196616 | tf_op jit(solution)/shard_map/ppermute | solution.py:109
  8.0 0.0 copy-start
  8.0 1.0 copy-done
  9.1 0.0 copy-start.2
  9.1 1.0 copy-done.2
  10.1 0.0 copy-start.1
  10.1 0.0 copy-start.3
  10.1 0.0 copy-start.4
  10.1 1.2 shard_map.46
  11.3 0.0 collective-permute-done
  11.3 14.9 %all_to_all.20 = bf16[4,64,512]{2,1,0:T(8,128)(2,1)} all-to-all(bf16[4,64,512]{2,1,0:T(8,128)(2,1)S(1)} %broadcast_in_dim.2), channel_id=1, replica_groups=mesh['x'=4,'z'=16,'y'=4,'c'=2] {'x'}, dimensions={0} | all-to-all | bytes 524288 | tf_op jit(solution)/shard_map/all_to_all | solution.py:122
  26.3 0.0 all-gather.3.cloned.1.call-update
  26.3 30.2 %all_to_all.21.s_ref = bf16[64,8,128]{2,1,0:T(8,128)(2,1)S(1)} all-to-all(bf16[64,8,128]{2,1,0:T(8,128)(2,1)S(1)} %bitcast.5), channel_id=1, replica_groups=mesh['x'=4,'z'=16,'y'=4,'c'=2] {'x','z'}, dimensions={0} | all-to-all | bytes 262144 | tf_op jit(solution)/shard_map/all_to_all | solution.py:126
  56.5 0.1 shard_map.47
  56.6 20.1 %all_to_all.22 = bf16[64,8,128]{2,1,0:T(8,128)(2,1)S(1)} all-to-all(bf16[64,8,128]{2,1,0:T(8,128)(2,1)S(1)} %shard_map.47), channel_id=1, replica_groups=mesh['x'=4,'z'=16,'y'=4,'c'=2] {'x','z'}, dimensions={0} | all-to-all | bytes 262144 | tf_op jit(solution)/shard_map/all_to_all | solution.py:130
  76.7 0.0 copy-done.1
  76.7 0.0 copy-done.3
  76.7 0.0 copy-done.4
  76.7 3.5 %shard_map.48 = bf16[4,512,512]{2,1,0:T(8,128)(2,1)S(1)} custom-call(bf16[512,512]{1,0:T(8,128)(2,1)S(1)} %copy-done.4, bf16[512,512]{1,0:T(8,128)(2,1)S(1)} %copy-done.1, bf16[512,512]{1,0:T(8,128)(2,1)S(1)} %copy-done.3, bf16[512,128]{1,0:T(8,128)(2,1)S(1)} %bitcast.6), custom_call_target="tpu_custom_call" | custom-call | tf_op jit(solution)/shard_map/pallas_call | solution.py:131
  80.2 22.8 %all_to_all.23.own_ref = bf16[4,512,512]{2,1,0:T(8,128)(2,1)S(1)} all-to-all(bf16[4,512,512]{2,1,0:T(8,128)(2,1)S(1)} %shard_map.48), channel_id=1, replica_groups=mesh['x'=4,'z'=16,'y'=4,'c'=2] {'y'}, dimensions={0} | all-to-all | bytes 4194304 | tf_op jit(solution)/shard_map/all_to_all | solution.py:139
  103.0 9.4 %collective-permute-start.1 = (bf16[4,512,512]{2,1,0:T(8,128)(2,1)S(1)}, bf16[4,512,512]{2,1,0:T(8,128)(2,1)}, u32[]{:S(2)}, u32[]{:S(2)}) collective-permute-start(bf16[4,512,512]{2,1,0:T(8,128)(2,1)S(1)} %all_to_all.23.own_ref), channel_id=1, source_target_pairs={{0,1},{1,0},{2,3},{3,2},{4,5},{5,4},{6,7},{7,6},{8,9},{9,8},{10,11... | collective-permute-start | bytes 6291464 | tf_op jit(solution)/shard_map/ppermute | solution.py:140
  112.4 3.9 %collective-permute-done.1.other_ref = bf16[4,512,512]{2,1,0:T(8,128)(2,1)} collective-permute-done((bf16[4,512,512]{2,1,0:T(8,128)(2,1)S(1)}, bf16[4,512,512]{2,1,0:T(8,128)(2,1)}, u32[]{:S(2)}, u32[]{:S(2)}) %collective-permute-start.1) | collective-permute-done | bytes 2097184 | tf_op jit(solution)/shard_map/ppermute | solution.py:140
  116.3 0.4 all-gather.3.cloned.1.call-done
  116.7 6.3 %shard_map.49 = bf16[512,512]{1,0:T(8,128)(2,1)} custom-call(s32[1]{0:T(128)} %bitcast.core_ref, bf16[4,512,512]{2,1,0:T(8,128)(2,1)S(1)} %all_to_all.23.own_ref, bf16[4,512,512]{2,1,0:T(8,128)(2,1)} %collective-permute-done.1.other_ref, bf16[16,2,4,64,512]{4,3,2,1,0:T(8,128)(2,1)} %bitcast.7), custom_call_target="tpu_custom_call" | custom-call | tf_op jit(solution)/shard_map/pallas_call | solution.py:82
  (1 shorter events, 0.0 us)
Async XLA Ops:
  6.5 110.2 %all-gather.3.cloned.1.call-start = ((), (), s32[]{:S(2)}) async-start(), calls=%async_computation.4 | async-start | bytes 8650752 | tf_op jit(solution)/shard_map/all_gather | solution.py:124
  6.5 4.8 %collective-permute-start = (bf16[64,512]{1,0:T(8,128)(2,1)}, bf16[64,512]{1,0:T(8,128)(2,1)S(1)}, u32[]{:S(2)}, u32[]{:S(2)}) collective-permute-start(bf16[64,512]{1,0:T(8,128)(2,1)} %bitcast.8), channel_id=1, source_target_pairs={{0,0},{2,128},{4,256},{6,384},{128,2},{130,130},{132,258},{134,386... | collective-permute-start | bytes 196616 | tf_op jit(solution)/shard_map/ppermute | solution.py:109
  8.0 1.0 copy-start
  9.1 1.0 copy-start.2
  10.1 66.5 %copy-start.1 = (bf16[512,512]{1,0:T(8,128)(2,1)S(1)}, bf16[512,512]{1,0:T(8,128)(2,1)}, u32[]{:S(2)}) copy-start(bf16[512,512]{1,0:T(8,128)(2,1)} %k_ref.3) | copy-start | bytes 1572868
  10.1 66.5 %copy-start.3 = (bf16[512,512]{1,0:T(8,128)(2,1)S(1)}, bf16[512,512]{1,0:T(8,128)(2,1)}, u32[]{:S(2)}) copy-start(bf16[512,512]{1,0:T(8,128)(2,1)} %v_ref.3) | copy-start | bytes 1572868
  10.1 66.6 %copy-start.4 = (bf16[512,512]{1,0:T(8,128)(2,1)S(1)}, bf16[512,512]{1,0:T(8,128)(2,1)}, u32[]{:S(2)}) copy-start(bf16[512,512]{1,0:T(8,128)(2,1)} %q_ref.1) | copy-start | bytes 1572868
  103.0 13.3 %collective-permute-start.1 = (bf16[4,512,512]{2,1,0:T(8,128)(2,1)S(1)}, bf16[4,512,512]{2,1,0:T(8,128)(2,1)}, u32[]{:S(2)}, u32[]{:S(2)}) collective-permute-start(bf16[4,512,512]{2,1,0:T(8,128)(2,1)S(1)} %all_to_all.23.own_ref), channel_id=1, source_target_pairs={{0,1},{1,0},{2,3},{3,2},{4,5},{5,4},{6,7},{7,6},{8,9},{9,8},{10,11... | collective-permute-start | bytes 6291464 | tf_op jit(solution)/shard_map/ppermute | solution.py:140
Sparse Core Ops, SparseCore 0:
  26.4 90.2 all-gather.2

commit v5 on v4

--- a/solution.py
+++ b/solution.py
@@ -8,6 +8,7 @@
 HEAD_DIM = 128
 NX, NZ, NY, NC = 4, 16, 4, 2
 N_CTX = NX * NZ
+HOME = 2
 BF = jnp.bfloat16
 F32 = jnp.float32
 
@@ -60,7 +61,7 @@
     def part(h_ref):
         total = None
         for y in range(sources):
-            w = w_ref[:, 0, y].reshape(blocks * cols, depth)
+            w = w_ref[:, 0, (y + HOME) % NX].reshape(blocks * cols, depth)
             one = lax.dot_general(h_ref[y], w, (((1,), (1,)), ((), ())), preferred_element_type=F32)
             total = one if total is None else total + one
         return total
@@ -77,7 +78,7 @@
 def project(core, own, other, w_all):
     sources, rows, depth = own.shape
     cols = w_all.shape[3]
-    zb = 4
+    zb = 8
     steps = NZ // NC // zb
     return pl.pallas_call(
         projection_kernel,
@@ -108,7 +109,7 @@
 
     w = lax.ppermute(
         out_weight.T, ("x", "y"),
-        [(x * NY + y, y * NY + x) for x in range(NX) for y in range(NY)],
+        [(x * NY + y, (y + HOME) % NX * NY + x) for x in range(NX) for y in range(NY)],
     )
     by_head = pl.BlockSpec((rows, HEAD_DIM), lambda h: (0, h))
     state = pl.BlockSpec((HEAD_DIM, HEAD_DIM), lambda h: (h, 0))

time: 130 us -> 128 us (0.985)
  blocking collectives: 88.1 us -> 83.8 us
  starting transfers between devices: 10.9 us -> 14.1 us
    all_to_all x1, blocking collectives: 14.9 us -> 10.4 us  [local(): w4 = lax.all_to_all(jnp.broadcast_to(w[None], (NX,) + w.shape), 'x', 0, 0)]
    ppermute x1, starting transfers between devices: 1.49 us -> 5.47 us  [local(): lax.ppermute(out_weight.T, ('x', 'y'), [(x * NY + y, (y + HOME) % NX * NY...]
where the time goes in v5:
time: 128 us
  blocking collectives  83.8 us (65%)
  starting transfers between devices  14.1 us (11%)
  between operations  13.5 us (11%)
  Pallas kernels  10.3 us (8%)
  waiting for transfers between devices  4.23 us (3%)
  local copies, waits for them, and re-layouts  2.11 us (2%)
    all_to_all x1, blocking collectives, local(): lax.all_to_all(states.reshape(N_CTX, part, HEAD_DIM), ('x', 'z'), 0, 0)  30.2 us
    all_to_all x1, blocking collectives, local(): hidden = lax.all_to_all(hidden, 'y', 0, 0)  23.5 us
    all_to_all x1, blocking collectives, local(): prefix = lax.all_to_all(scanned, ('x', 'z'), 0, 0).reshape(width, HEAD_DIM)  19.7 us
    all_to_all x1, blocking collectives, local(): w4 = lax.all_to_all(jnp.broadcast_to(w[None], (NX,) + w.shape), 'x', 0, 0)  10.4 us
    ppermute x1, starting transfers between devices, local(): other = lax.ppermute(hidden, 'c', [(0, 1), (1, 0)])  8.65 us
    pallas_call x1, Pallas kernels, project(): pl.pallas_call(projection_kernel, grid_spec=pltpu.PrefetchScalarGridSpec(...  5.6 us
    ppermute x1, starting transfers between devices, local(): lax.ppermute(out_weight.T, ('x', 'y'), [(x * NY + y, (y + HOME) % NX * NY...  5.47 us
    ppermute x1, waiting for transfers between devices, local(): other = lax.ppermute(hidden, 'c', [(0, 1), (1, 0)])  3.89 us
  transfers between devices with their start and end apart: 3, of which 2 were waited for; matrix products, arithmetic and copies ran while one was open for 0% of the time, Pallas kernels for 4%

profile of v5, /device:TPU:1, one launch (start us, length us, event | category | flops | bytes accessed | tf_op | source)
XLA Modules:
  0.0 128.1 jit_solution(2186201993681577285)
XLA Ops:
  6.5 0.0 all-gather.3.cloned.1.call-start
  6.5 5.5 %collective-permute-start = (bf16[64,512]{1,0:T(8,128)(2,1)}, bf16[64,512]{1,0:T(8,128)(2,1)S(1)}, u32[]{:S(2)}, u32[]{:S(2)}) collective-permute-start(bf16[64,512]{1,0:T(8,128)(2,1)} %bitcast.8), channel_id=1, source_target_pairs={{0,256},{2,384},{4,0},{6,128},{128,258},{130,386},{132,2},{134,130... | collective-permute-start | bytes 196616 | tf_op jit(solution)/shard_map/ppermute | solution.py:110
  12.0 0.0 copy-start
  12.0 1.0 copy-done
  13.1 0.0 copy-start.2
  13.1 1.0 copy-done.2
  14.1 0.0 copy-start.1
  14.1 0.0 copy-start.3
  14.1 0.0 copy-start.4
  14.1 1.2 shard_map.46
  15.3 0.0 collective-permute-done
  15.3 10.4 %all_to_all.20 = bf16[4,64,512]{2,1,0:T(8,128)(2,1)} all-to-all(bf16[4,64,512]{2,1,0:T(8,128)(2,1)S(1)} %broadcast_in_dim.2), channel_id=1, replica_groups=mesh['x'=4,'z'=16,'y'=4,'c'=2] {'x'}, dimensions={0} | all-to-all | bytes 524288 | tf_op jit(solution)/shard_map/all_to_all | solution.py:123
  25.8 0.0 all-gather.3.cloned.1.call-update
  25.8 30.2 %all_to_all.21.s_ref = bf16[64,8,128]{2,1,0:T(8,128)(2,1)S(1)} all-to-all(bf16[64,8,128]{2,1,0:T(8,128)(2,1)S(1)} %bitcast.5), channel_id=1, replica_groups=mesh['x'=4,'z'=16,'y'=4,'c'=2] {'x','z'}, dimensions={0} | all-to-all | bytes 262144 | tf_op jit(solution)/shard_map/all_to_all | solution.py:127
  56.0 0.1 shard_map.47
  56.1 19.7 %all_to_all.22 = bf16[64,8,128]{2,1,0:T(8,128)(2,1)S(1)} all-to-all(bf16[64,8,128]{2,1,0:T(8,128)(2,1)S(1)} %shard_map.47), channel_id=1, replica_groups=mesh['x'=4,'z'=16,'y'=4,'c'=2] {'x','z'}, dimensions={0} | all-to-all | bytes 262144 | tf_op jit(solution)/shard_map/all_to_all | solution.py:131
  75.8 0.0 copy-done.1
  75.8 0.0 copy-done.3
  75.8 0.0 copy-done.4
  75.8 3.5 %shard_map.48 = bf16[4,512,512]{2,1,0:T(8,128)(2,1)S(1)} custom-call(bf16[512,512]{1,0:T(8,128)(2,1)S(1)} %copy-done.4, bf16[512,512]{1,0:T(8,128)(2,1)S(1)} %copy-done.1, bf16[512,512]{1,0:T(8,128)(2,1)S(1)} %copy-done.3, bf16[512,128]{1,0:T(8,128)(2,1)S(1)} %bitcast.6), custom_call_target="tpu_custom_call" | custom-call | tf_op jit(solution)/shard_map/pallas_call | solution.py:132
  79.3 23.5 %all_to_all.23.own_ref = bf16[4,512,512]{2,1,0:T(8,128)(2,1)S(1)} all-to-all(bf16[4,512,512]{2,1,0:T(8,128)(2,1)S(1)} %shard_map.48), channel_id=1, replica_groups=mesh['x'=4,'z'=16,'y'=4,'c'=2] {'y'}, dimensions={0} | all-to-all | bytes 4194304 | tf_op jit(solution)/shard_map/all_to_all | solution.py:140
  102.8 8.7 %collective-permute-start.1 = (bf16[4,512,512]{2,1,0:T(8,128)(2,1)S(1)}, bf16[4,512,512]{2,1,0:T(8,128)(2,1)}, u32[]{:S(2)}, u32[]{:S(2)}) collective-permute-start(bf16[4,512,512]{2,1,0:T(8,128)(2,1)S(1)} %all_to_all.23.own_ref), channel_id=1, source_target_pairs={{0,1},{1,0},{2,3},{3,2},{4,5},{5,4},{6,7},{7,6},{8,9},{9,8},{10,11... | collective-permute-start | bytes 6291464 | tf_op jit(solution)/shard_map/ppermute | solution.py:141
  111.5 3.9 %collective-permute-done.1.other_ref = bf16[4,512,512]{2,1,0:T(8,128)(2,1)} collective-permute-done((bf16[4,512,512]{2,1,0:T(8,128)(2,1)S(1)}, bf16[4,512,512]{2,1,0:T(8,128)(2,1)}, u32[]{:S(2)}, u32[]{:S(2)}) %collective-permute-start.1) | collective-permute-done | bytes 2097184 | tf_op jit(solution)/shard_map/ppermute | solution.py:141
  115.4 0.3 all-gather.3.cloned.1.call-done
  115.7 5.6 %shard_map.49 = bf16[512,512]{1,0:T(8,128)(2,1)} custom-call(s32[1]{0:T(128)} %bitcast.core_ref, bf16[4,512,512]{2,1,0:T(8,128)(2,1)S(1)} %all_to_all.23.own_ref, bf16[4,512,512]{2,1,0:T(8,128)(2,1)} %collective-permute-done.1.other_ref, bf16[16,2,4,64,512]{4,3,2,1,0:T(8,128)(2,1)} %bitcast.7), custom_call_target="tpu_custom_call" | custom-call | tf_op jit(solution)/shard_map/pallas_call | solution.py:83
  (1 shorter events, 0.0 us)
Async XLA Ops:
  6.5 109.1 %all-gather.3.cloned.1.call-start = ((), (), s32[]{:S(2)}) async-start(), calls=%async_computation.4 | async-start | bytes 8650752 | tf_op jit(solution)/shard_map/all_gather | solution.py:125
  6.5 8.7 %collective-permute-start = (bf16[64,512]{1,0:T(8,128)(2,1)}, bf16[64,512]{1,0:T(8,128)(2,1)S(1)}, u32[]{:S(2)}, u32[]{:S(2)}) collective-permute-start(bf16[64,512]{1,0:T(8,128)(2,1)} %bitcast.8), channel_id=1, source_target_pairs={{0,256},{2,384},{4,0},{6,128},{128,258},{130,386},{132,2},{134,130... | collective-permute-start | bytes 196616 | tf_op jit(solution)/shard_map/ppermute | solution.py:110
  12.0 1.0 copy-start
  13.1 1.0 copy-start.2
  14.1 61.7 %copy-start.1 = (bf16[512,512]{1,0:T(8,128)(2,1)S(1)}, bf16[512,512]{1,0:T(8,128)(2,1)}, u32[]{:S(2)}) copy-start(bf16[512,512]{1,0:T(8,128)(2,1)} %k_ref.3) | copy-start | bytes 1572868
  14.1 61.7 %copy-start.3 = (bf16[512,512]{1,0:T(8,128)(2,1)S(1)}, bf16[512,512]{1,0:T(8,128)(2,1)}, u32[]{:S(2)}) copy-start(bf16[512,512]{1,0:T(8,128)(2,1)} %v_ref.3) | copy-start | bytes 1572868
  14.1 61.7 %copy-start.4 = (bf16[512,512]{1,0:T(8,128)(2,1)S(1)}, bf16[512,512]{1,0:T(8,128)(2,1)}, u32[]{:S(2)}) copy-start(bf16[512,512]{1,0:T(8,128)(2,1)} %q_ref.1) | copy-start | bytes 1572868
  102.8 12.6 %collective-permute-start.1 = (bf16[4,512,512]{2,1,0:T(8,128)(2,1)S(1)}, bf16[4,512,512]{2,1,0:T(8,128)(2,1)}, u32[]{:S(2)}, u32[]{:S(2)}) collective-permute-start(bf16[4,512,512]{2,1,0:T(8,128)(2,1)S(1)} %all_to_all.23.own_ref), channel_id=1, source_target_pairs={{0,1},{1,0},{2,3},{3,2},{4,5},{5,4},{6,7},{7,6},{8,9},{9,8},{10,11... | collective-permute-start | bytes 6291464 | tf_op jit(solution)/shard_map/ppermute | solution.py:141
Sparse Core Ops, SparseCore 0:
  25.9 89.7 all-gather.2

commit v6 on v5

--- a/solution.py
+++ b/solution.py
@@ -55,46 +55,58 @@
             o_ref[n, here, :] = hidden
 
 
-def projection_kernel(core_ref, own_ref, other_ref, w_ref, o_ref, acc_ref):
-    blocks, _, sources, cols, depth = w_ref.shape
-
-    def part(h_ref):
+def projection_kernel(core_ref, own_ref, far_ref, w_ref, o_ref, *scratch):
+    parts, other_ref, acc_ref, sem = scratch[:4], scratch[4], scratch[5], scratch[6]
+    core = core_ref[0]
+    blocks, _, per, cols, depth = parts[0].shape
+    rows_of = [(k, first) for k in range(NC) for first in range(0, NY, per)]
+    copies = [
+        pltpu.make_async_copy(
+            w_ref.at[pl.ds(core * blocks, blocks), pl.ds(core ^ k, 1), pl.ds(first, per)], part, sem.at[n]
+        )
+        for n, ((k, first), part) in enumerate(zip(rows_of, parts))
+    ]
+    other = pltpu.make_async_copy(far_ref, other_ref, sem.at[len(copies)])
+    copies[0].start()
+    copies[1].start()
+    other.start()
+    copies[2].start()
+    copies[3].start()
+    for n, (k, first) in enumerate(rows_of):
+        copies[n].wait()
+        if n == len(rows_of) // NC:
+            other.wait()
+        h_ref = own_ref if k == 0 else other_ref
         total = None
-        for y in range(sources):
-            w = w_ref[:, 0, (y + HOME) % NX].reshape(blocks * cols, depth)
-            one = lax.dot_general(h_ref[y], w, (((1,), (1,)), ((), ())), preferred_element_type=F32)
+        for i in range(per):
+            w = parts[n][:, 0, i].reshape(blocks * cols, depth)
+            one = lax.dot_general(
+                h_ref[(first + i - HOME) % NY], w, (((1,), (1,)), ((), ())), preferred_element_type=F32
+            )
             total = one if total is None else total + one
-        return total
-
-    @pl.when(pl.program_id(1) == 0)
-    def _():
-        acc_ref[...] = part(own_ref)
-
-    @pl.when(pl.program_id(1) == 1)
-    def _():
-        o_ref[...] = (acc_ref[...] + part(other_ref)).astype(o_ref.dtype)
+        if n == 0:
+            acc_ref[...] = total
+        elif n < len(rows_of) - 1:
+            acc_ref[...] += total
+        else:
+            o_ref[...] = (acc_ref[...] + total).astype(o_ref.dtype)
 
 
 def project(core, own, other, w_all):
     sources, rows, depth = own.shape
     cols = w_all.shape[3]
-    zb = 8
-    steps = NZ // NC // zb
+    blocks, per = NZ // NC, NY // 2
+    anywhere, vmem = pl.BlockSpec(memory_space=pl.ANY), pl.BlockSpec(memory_space=pltpu.VMEM)
     return pl.pallas_call(
         projection_kernel,
-        grid_spec=pltpu.PrefetchScalarGridSpec(
-            num_scalar_prefetch=1,
-            grid=(steps, NC),
-            in_specs=[pl.BlockSpec(memory_space=pltpu.VMEM)] * 2 + [
-                pl.BlockSpec(
-                    (zb, 1, sources, cols, depth),
-                    lambda n, k, core: (core[0] * steps + n, core[0] ^ k, 0, 0, 0),
-                ),
-            ],
-            out_specs=pl.BlockSpec((rows, zb * cols), lambda n, k, core: (0, n)),
-            scratch_shapes=[pltpu.VMEM((rows, zb * cols), F32)],
-        ),
-        out_shape=jax.ShapeDtypeStruct((rows, NZ // NC * cols), BF),
+        in_specs=[pl.BlockSpec(memory_space=pltpu.SMEM), vmem, anywhere, anywhere],
+        out_specs=vmem,
+        scratch_shapes=[pltpu.VMEM((blocks, 1, per, cols, depth), BF)] * 4 + [
+            pltpu.VMEM((sources, rows, depth), BF),
+            pltpu.VMEM((rows, blocks * cols), F32),
+            pltpu.SemaphoreType.DMA((5,)),
+        ],
+        out_shape=jax.ShapeDtypeStruct((rows, blocks * cols), BF),
         compiler_params=params(),
     )(core, own, other, w_all)
 

time: 128 us -> 128 us (level)
  no operation moved by 1% of the time
where the time goes in v6:
time: 128 us; the launch traced here: 127 us
  blocking collectives  83.8 us (65%)
  starting transfers between devices  14.1 us (11%)
  between operations  13.5 us (11%)
  Pallas kernels  9.44 us (7%)
  waiting for transfers between devices  4.23 us (3%)
  local copies, waits for them, and re-layouts  2.11 us (2%)
    all_to_all x1, blocking collectives, local(): lax.all_to_all(states.reshape(N_CTX, part, HEAD_DIM), ('x', 'z'), 0, 0)  30.2 us
    all_to_all x1, blocking collectives, local(): hidden = lax.all_to_all(hidden, 'y', 0, 0)  23.5 us
    all_to_all x1, blocking collectives, local(): prefix = lax.all_to_all(scanned, ('x', 'z'), 0, 0).reshape(width, HEAD_DIM)  19.7 us
    all_to_all x1, blocking collectives, local(): w4 = lax.all_to_all(jnp.broadcast_to(w[None], (NX,) + w.shape), 'x', 0, 0)  10.4 us
    ppermute x1, starting transfers between devices, local(): other = lax.ppermute(hidden, 'c', [(0, 1), (1, 0)])  8.65 us
    ppermute x1, starting transfers between devices, local(): lax.ppermute(out_weight.T, ('x', 'y'), [(x * NY + y, (y + HOME) % NX * NY...  5.47 us
    pallas_call x1, Pallas kernels, project(): pl.pallas_call(projection_kernel, in_specs=[pl.BlockSpec(memory_space=plt...  4.68 us
    ppermute x1, waiting for transfers between devices, local(): other = lax.ppermute(hidden, 'c', [(0, 1), (1, 0)])  3.89 us
  transfers between devices with their start and end apart: 3, of which 2 were waited for; matrix products, arithmetic and copies ran while one was open for 0% of the time, Pallas kernels for 4%

profile of v6, /device:TPU:1, one launch (start us, length us, event | category | flops | bytes accessed | tf_op | source)
XLA Modules:
  0.0 127.2 jit_solution(11921768689448530794)
XLA Ops:
  6.5 0.0 all-gather.3.cloned.1.call-start
  6.5 5.5 %collective-permute-start = (bf16[64,512]{1,0:T(8,128)(2,1)}, bf16[64,512]{1,0:T(8,128)(2,1)S(1)}, u32[]{:S(2)}, u32[]{:S(2)}) collective-permute-start(bf16[64,512]{1,0:T(8,128)(2,1)} %bitcast.8), channel_id=1, source_target_pairs={{0,256},{2,384},{4,0},{6,128},{128,258},{130,386},{132,2},{134,130... | collective-permute-start | bytes 196616 | tf_op jit(solution)/shard_map/ppermute | solution.py:122
  12.0 0.0 copy-start
  12.0 1.0 copy-done
  13.1 0.0 copy-start.2
  13.1 1.0 copy-done.2
  14.1 0.0 copy-start.1
  14.1 0.0 copy-start.3
  14.1 0.0 copy-start.4
  14.1 1.2 shard_map.46
  15.3 0.0 collective-permute-done
  15.3 10.4 %all_to_all.20 = bf16[4,64,512]{2,1,0:T(8,128)(2,1)} all-to-all(bf16[4,64,512]{2,1,0:T(8,128)(2,1)S(1)} %broadcast_in_dim.2), channel_id=1, replica_groups=mesh['x'=4,'z'=16,'y'=4,'c'=2] {'x'}, dimensions={0} | all-to-all | bytes 524288 | tf_op jit(solution)/shard_map/all_to_all | solution.py:135
  25.8 0.0 all-gather.3.cloned.1.call-update
  25.8 30.2 %all_to_all.21.s_ref = bf16[64,8,128]{2,1,0:T(8,128)(2,1)S(1)} all-to-all(bf16[64,8,128]{2,1,0:T(8,128)(2,1)S(1)} %bitcast.5), channel_id=1, replica_groups=mesh['x'=4,'z'=16,'y'=4,'c'=2] {'x','z'}, dimensions={0} | all-to-all | bytes 262144 | tf_op jit(solution)/shard_map/all_to_all | solution.py:139
  56.0 0.1 shard_map.47
  56.1 19.7 %all_to_all.22 = bf16[64,8,128]{2,1,0:T(8,128)(2,1)S(1)} all-to-all(bf16[64,8,128]{2,1,0:T(8,128)(2,1)S(1)} %shard_map.47), channel_id=1, replica_groups=mesh['x'=4,'z'=16,'y'=4,'c'=2] {'x','z'}, dimensions={0} | all-to-all | bytes 262144 | tf_op jit(solution)/shard_map/all_to_all | solution.py:143
  75.8 0.0 copy-done.1
  75.8 0.0 copy-done.3
  75.8 0.0 copy-done.4
  75.8 3.5 %shard_map.48 = bf16[4,512,512]{2,1,0:T(8,128)(2,1)S(1)} custom-call(bf16[512,512]{1,0:T(8,128)(2,1)S(1)} %copy-done.4, bf16[512,512]{1,0:T(8,128)(2,1)S(1)} %copy-done.1, bf16[512,512]{1,0:T(8,128)(2,1)S(1)} %copy-done.3, bf16[512,128]{1,0:T(8,128)(2,1)S(1)} %bitcast.6), custom_call_target="tpu_custom_call" | custom-call | tf_op jit(solution)/shard_map/pallas_call | solution.py:144
  79.3 23.5 %all_to_all.23.own_ref = bf16[4,512,512]{2,1,0:T(8,128)(2,1)S(1)} all-to-all(bf16[4,512,512]{2,1,0:T(8,128)(2,1)S(1)} %shard_map.48), channel_id=1, replica_groups=mesh['x'=4,'z'=16,'y'=4,'c'=2] {'y'}, dimensions={0} | all-to-all | bytes 4194304 | tf_op jit(solution)/shard_map/all_to_all | solution.py:152
  102.8 8.7 %collective-permute-start.1 = (bf16[4,512,512]{2,1,0:T(8,128)(2,1)S(1)}, bf16[4,512,512]{2,1,0:T(8,128)(2,1)}, u32[]{:S(2)}, u32[]{:S(2)}) collective-permute-start(bf16[4,512,512]{2,1,0:T(8,128)(2,1)S(1)} %all_to_all.23.own_ref), channel_id=1, source_target_pairs={{0,1},{1,0},{2,3},{3,2},{4,5},{5,4},{6,7},{7,6},{8,9},{9,8},{10,11... | collective-permute-start | bytes 6291464 | tf_op jit(solution)/shard_map/ppermute | solution.py:153
  111.5 3.9 %collective-permute-done.1.far_ref = bf16[4,512,512]{2,1,0:T(8,128)(2,1)} collective-permute-done((bf16[4,512,512]{2,1,0:T(8,128)(2,1)S(1)}, bf16[4,512,512]{2,1,0:T(8,128)(2,1)}, u32[]{:S(2)}, u32[]{:S(2)}) %collective-permute-start.1) | collective-permute-done | bytes 2097184 | tf_op jit(solution)/shard_map/ppermute | solution.py:153
  115.4 0.3 all-gather.3.cloned.1.call-done
  115.7 4.7 %shard_map.49 = bf16[512,512]{1,0:T(8,128)(2,1)} custom-call(s32[1]{0:T(128)} %bitcast.core_ref, bf16[4,512,512]{2,1,0:T(8,128)(2,1)S(1)} %all_to_all.23.own_ref, bf16[4,512,512]{2,1,0:T(8,128)(2,1)} %collective-permute-done.1.far_ref, bf16[16,2,4,64,512]{4,3,2,1,0:T(8,128)(2,1)} %bitcast.7), custom_call_target="tpu_custom_call" | custom-call | tf_op jit(solution)/shard_map/pallas_call | solution.py:100
  (1 shorter events, 0.0 us)
Async XLA Ops:
  6.5 109.1 %all-gather.3.cloned.1.call-start = ((), (), s32[]{:S(2)}) async-start(), calls=%async_computation.4 | async-start | bytes 8650752 | tf_op jit(solution)/shard_map/all_gather | solution.py:137
  6.5 8.7 %collective-permute-start = (bf16[64,512]{1,0:T(8,128)(2,1)}, bf16[64,512]{1,0:T(8,128)(2,1)S(1)}, u32[]{:S(2)}, u32[]{:S(2)}) collective-permute-start(bf16[64,512]{1,0:T(8,128)(2,1)} %bitcast.8), channel_id=1, source_target_pairs={{0,256},{2,384},{4,0},{6,128},{128,258},{130,386},{132,2},{134,130... | collective-permute-start | bytes 196616 | tf_op jit(solution)/shard_map/ppermute | solution.py:122
  12.0 1.0 copy-start
  13.1 1.0 copy-start.2
  14.1 61.7 %copy-start.1 = (bf16[512,512]{1,0:T(8,128)(2,1)S(1)}, bf16[512,512]{1,0:T(8,128)(2,1)}, u32[]{:S(2)}) copy-start(bf16[512,512]{1,0:T(8,128)(2,1)} %k_ref.3) | copy-start | bytes 1572868
  14.1 61.7 %copy-start.3 = (bf16[512,512]{1,0:T(8,128)(2,1)S(1)}, bf16[512,512]{1,0:T(8,128)(2,1)}, u32[]{:S(2)}) copy-start(bf16[512,512]{1,0:T(8,128)(2,1)} %v_ref.3) | copy-start | bytes 1572868
  14.1 61.7 %copy-start.4 = (bf16[512,512]{1,0:T(8,128)(2,1)S(1)}, bf16[512,512]{1,0:T(8,128)(2,1)}, u32[]{:S(2)}) copy-start(bf16[512,512]{1,0:T(8,128)(2,1)} %q_ref.1) | copy-start | bytes 1572868
  102.8 12.6 %collective-permute-start.1 = (bf16[4,512,512]{2,1,0:T(8,128)(2,1)S(1)}, bf16[4,512,512]{2,1,0:T(8,128)(2,1)}, u32[]{:S(2)}, u32[]{:S(2)}) collective-permute-start(bf16[4,512,512]{2,1,0:T(8,128)(2,1)S(1)} %all_to_all.23.own_ref), channel_id=1, source_target_pairs={{0,1},{1,0},{2,3},{3,2},{4,5},{5,4},{6,7},{7,6},{8,9},{9,8},{10,11... | collective-permute-start | bytes 6291464 | tf_op jit(solution)/shard_map/ppermute | solution.py:153
Sparse Core Ops, SparseCore 0:
  25.9 89.7 all-gather.2

commit v7 on v6

--- a/solution.py
+++ b/solution.py
@@ -30,33 +30,37 @@
         total = total + s_ref[c].astype(F32)
 
 
-def attention_kernel(q_ref, k_ref, v_ref, p_ref, o_ref):
+def intra_kernel(q_ref, k_ref, v_ref, o_ref):
     rows = q_ref.shape[0]
     blk = 256
     t = lax.broadcasted_iota(jnp.int32, (blk, blk), 0)
     s = lax.broadcasted_iota(jnp.int32, (blk, blk), 1)
     causal = t >= s
-    prefix = p_ref[...]
     for i in range(rows // blk):
         here = slice(i * blk, (i + 1) * blk)
-        q = q_ref[here, :]
-        attn = jnp.dot(q, prefix, preferred_element_type=F32)
+        attn = None
         for j in range(i + 1):
             there = slice(j * blk, (j + 1) * blk)
             scores = lax.dot_general(
-                q, k_ref[there, :], (((1,), (1,)), ((), ())), preferred_element_type=F32
+                q_ref[here, :], k_ref[there, :], (((1,), (1,)), ((), ())), preferred_element_type=F32
             )
             if i == j:
                 scores = jnp.where(causal, scores, 0.0)
-            attn += jnp.dot(scores.astype(BF), v_ref[there, :], preferred_element_type=F32)
-        scale = lax.rsqrt(jnp.mean(attn * attn, axis=-1, keepdims=True) + 1e-06)
-        hidden = (attn * scale).astype(BF)
-        for n in range(o_ref.shape[0]):
-            o_ref[n, here, :] = hidden
+            part = jnp.dot(scores.astype(BF), v_ref[there, :], preferred_element_type=F32)
+            attn = part if attn is None else attn + part
+        o_ref[here, :] = attn
+
+
+def attention_kernel(q_ref, i_ref, p_ref, o_ref):
+    attn = i_ref[...] + jnp.dot(q_ref[...], p_ref[...], preferred_element_type=F32)
+    scale = lax.rsqrt(jnp.mean(attn * attn, axis=-1, keepdims=True) + 1e-06)
+    hidden = (attn * scale).astype(BF)
+    for n in range(o_ref.shape[0]):
+        o_ref[n] = hidden
 
 
 def projection_kernel(core_ref, own_ref, far_ref, w_ref, o_ref, *scratch):
-    parts, other_ref, acc_ref, sem = scratch[:4], scratch[4], scratch[5], scratch[6]
+    parts, (other_ref, acc_ref, out_ref, sem) = scratch[:4], scratch[4:]
     core = core_ref[0]
     blocks, _, per, cols, depth = parts[0].shape
     rows_of = [(k, first) for k in range(NC) for first in range(0, NY, per)]
@@ -67,29 +71,36 @@
         for n, ((k, first), part) in enumerate(zip(rows_of, parts))
     ]
     other = pltpu.make_async_copy(far_ref, other_ref, sem.at[len(copies)])
+    halves = (pl.ds(0, o_ref.shape[0] // 2), pl.ds(o_ref.shape[0] // 2, o_ref.shape[0] // 2))
+    outs = [pltpu.make_async_copy(out_ref.at[r], o_ref.at[r], sem.at[5 + n]) for n, r in enumerate(halves)]
     copies[0].start()
     copies[1].start()
     other.start()
     copies[2].start()
     copies[3].start()
+    half = own_ref.shape[1] // 2
     for n, (k, first) in enumerate(rows_of):
         copies[n].wait()
         if n == len(rows_of) // NC:
             other.wait()
         h_ref = own_ref if k == 0 else other_ref
-        total = None
-        for i in range(per):
-            w = parts[n][:, 0, i].reshape(blocks * cols, depth)
-            one = lax.dot_general(
-                h_ref[(first + i - HOME) % NY], w, (((1,), (1,)), ((), ())), preferred_element_type=F32
-            )
-            total = one if total is None else total + one
-        if n == 0:
-            acc_ref[...] = total
-        elif n < len(rows_of) - 1:
-            acc_ref[...] += total
-        else:
-            o_ref[...] = (acc_ref[...] + total).astype(o_ref.dtype)
+        last = n == len(rows_of) - 1
+        for rows in (slice(0, half), slice(half, 2 * half)) if last else (slice(0, 2 * half),):
+            total = None
+            for i in range(per):
+                w = parts[n][:, 0, i].reshape(blocks * cols, depth)
+                h = h_ref[(first + i - HOME) % NY, rows]
+                one = lax.dot_general(h, w, (((1,), (1,)), ((), ())), preferred_element_type=F32)
+                total = one if total is None else total + one
+            if n == 0:
+                acc_ref[...] = total
+            elif not last:
+                acc_ref[...] += total
+            else:
+                out_ref[rows, :] = (acc_ref[rows, :] + total).astype(o_ref.dtype)
+                outs[rows.start // half].start()
+    for out in outs:
+        out.wait()
 
 
 def project(core, own, other, w_all):
@@ -100,11 +111,12 @@
     return pl.pallas_call(
         projection_kernel,
         in_specs=[pl.BlockSpec(memory_space=pltpu.SMEM), vmem, anywhere, anywhere],
-        out_specs=vmem,
+        out_specs=anywhere,
         scratch_shapes=[pltpu.VMEM((blocks, 1, per, cols, depth), BF)] * 4 + [
             pltpu.VMEM((sources, rows, depth), BF),
             pltpu.VMEM((rows, blocks * cols), F32),
-            pltpu.SemaphoreType.DMA((5,)),
+            pltpu.VMEM((rows, blocks * cols), BF),
+            pltpu.SemaphoreType.DMA((7,)),
         ],
         out_shape=jax.ShapeDtypeStruct((rows, blocks * cols), BF),
         compiler_params=params(),
@@ -135,6 +147,16 @@
     w4 = lax.all_to_all(jnp.broadcast_to(w[None], (NX,) + w.shape), "x", 0, 0)
     states, w4 = lax.optimization_barrier((states, w4))
     w_all = lax.all_gather(w4, ("z", "c")).reshape((NZ, NC) + w4.shape)
+    intra = pl.pallas_call(
+        intra_kernel,
+        grid=(heads,),
+        out_shape=jax.ShapeDtypeStruct((rows, width), F32),
+        in_specs=[by_head] * 3, out_specs=by_head,
+        cost_estimate=pl.CostEstimate(
+            flops=4 * rows * rows * width, bytes_accessed=10 * rows * width, transcendentals=0
+        ),
+        compiler_params=params(),
+    )(queries, keys, values)
     part = width // N_CTX
     mine = lax.all_to_all(states.reshape(N_CTX, part, HEAD_DIM), ("x", "z"), 0, 0)
     scanned = pl.pallas_call(
@@ -145,10 +167,10 @@
         attention_kernel,
         grid=(heads,),
         out_shape=jax.ShapeDtypeStruct((NY, rows, width), BF),
-        in_specs=[by_head, by_head, by_head, state],
+        in_specs=[by_head, by_head, state],
         out_specs=pl.BlockSpec((NY, rows, HEAD_DIM), lambda h: (0, 0, h)),
         compiler_params=params(),
-    )(queries, keys, values, prefix)
+    )(queries, intra, prefix)
     hidden = lax.all_to_all(hidden, "y", 0, 0)
     other = lax.ppermute(hidden, "c", [(0, 1), (1, 0)])
     return project(me_c.astype(jnp.int32).reshape(1), hidden, other, w_all)

time: 128 us -> 127 us (level)
  blocking collectives: 83.8 us -> 63.8 us
  waiting for transfers between devices: 4.23 us -> 16.4 us
  starting transfers between devices: 14.1 us -> 20.3 us
  Pallas kernels: 9.44 us -> 10.9 us
    all_to_all x1 -> x0, blocking collectives: 19.7 us -> none  [local(): prefix = lax.all_to_all(scanned, ('x', 'z'), 0, 0).reshape(width, HEAD_DIM)]
    all_to_all x0 -> x1, waiting for transfers between devices: none -> 11.5 us  [local(): prefix = lax.all_to_all(scanned, ('x', 'z'), 0, 0).reshape(width, HEAD_DIM)]
    all_to_all x0 -> x1, starting transfers between devices: none -> 5.46 us  [local(): prefix = lax.all_to_all(scanned, ('x', 'z'), 0, 0).reshape(width, HEAD_DIM)]
    pallas_call x0 -> x1, Pallas kernels: none -> 2.58 us  [local(): pl.pallas_call(intra_kernel, grid=(heads,), out_shape=jax.ShapeDtypeStruc...]
    pallas_call x1, Pallas kernels: 3.52 us -> 1.81 us  [local(): pl.pallas_call(attention_kernel, grid=(heads,), out_shape=jax.ShapeDtypeS...]
  transfers between devices with their start and end apart: 3 -> 4, of which waited for: 2 -> 3; matrix products, arithmetic and copies ran while one was open for 0% -> 0% of each run, Pallas kernels for 4% -> 5%
where the time goes in v7:
time: 127 us
  blocking collectives  63.8 us (50%)
  starting transfers between devices  20.3 us (16%)
  waiting for transfers between devices  16.4 us (13%)
  between operations  13.5 us (11%)
  Pallas kernels  10.9 us (9%)
  local copies, waits for them, and re-layouts  2.11 us (2%)
    all_to_all x1, blocking collectives, local(): lax.all_to_all(states.reshape(N_CTX, part, HEAD_DIM), ('x', 'z'), 0, 0)  30.2 us
    all_to_all x1, blocking collectives, local(): hidden = lax.all_to_all(hidden, 'y', 0, 0)  23.1 us
    all_to_all x1, waiting for transfers between devices, local(): prefix = lax.all_to_all(scanned, ('x', 'z'), 0, 0).reshape(width, HEAD_DIM)  11.5 us
    all_to_all x1, blocking collectives, local(): w4 = lax.all_to_all(jnp.broadcast_to(w[None], (NX,) + w.shape), 'x', 0, 0)  10.4 us
    ppermute x1, starting transfers between devices, local(): other = lax.ppermute(hidden, 'c', [(0, 1), (1, 0)])  9.39 us
    ppermute x1, starting transfers between devices, local(): lax.ppermute(out_weight.T, ('x', 'y'), [(x * NY + y, (y + HOME) % NX * NY...  5.47 us
    all_to_all x1, starting transfers between devices, local(): prefix = lax.all_to_all(scanned, ('x', 'z'), 0, 0).reshape(width, HEAD_DIM)  5.46 us
    pallas_call x1, Pallas kernels, project(): pl.pallas_call(projection_kernel, in_specs=[pl.BlockSpec(memory_space=plt...  4.61 us
  transfers between devices with their start and end apart: 4, of which 3 were waited for; matrix products, arithmetic and copies ran while one was open for 0% of the time, Pallas kernels for 5%

profile of v7, /device:TPU:1, one launch (start us, length us, event | category | flops | bytes accessed | tf_op | source)
XLA Modules:
  0.0 127.0 jit_solution(12001846319418980753)
XLA Ops:
  6.5 0.0 all-gather.3.cloned.1.call-start
  6.5 5.5 %collective-permute-start = (bf16[64,512]{1,0:T(8,128)(2,1)}, bf16[64,512]{1,0:T(8,128)(2,1)S(1)}, u32[]{:S(2)}, u32[]{:S(2)}) collective-permute-start(bf16[64,512]{1,0:T(8,128)(2,1)} %bitcast.8), channel_id=1, source_target_pairs={{0,256},{2,384},{4,0},{6,128},{128,258},{130,386},{132,2},{134,130... | collective-permute-start | bytes 196616 | tf_op jit(solution)/shard_map/ppermute | solution.py:134
  12.0 0.0 copy-start
  12.0 1.0 copy-done
  13.1 0.0 copy-start.2
  13.1 1.0 copy-done.2
  14.1 0.0 copy-start.1
  14.1 0.0 copy-start.3
  14.1 0.0 copy-start.4
  14.1 1.2 shard_map.47
  15.3 0.0 collective-permute-done
  15.3 10.4 %all_to_all.20 = bf16[4,64,512]{2,1,0:T(8,128)(2,1)} all-to-all(bf16[4,64,512]{2,1,0:T(8,128)(2,1)S(1)} %broadcast_in_dim.2), channel_id=1, replica_groups=mesh['x'=4,'z'=16,'y'=4,'c'=2] {'x'}, dimensions={0} | all-to-all | bytes 524288 | tf_op jit(solution)/shard_map/all_to_all | solution.py:147
  25.8 0.0 all-gather.3.cloned.1.call-update
  25.8 30.2 %all_to_all.21.s_ref = bf16[64,8,128]{2,1,0:T(8,128)(2,1)S(1)} all-to-all(bf16[64,8,128]{2,1,0:T(8,128)(2,1)S(1)} %bitcast.5), channel_id=1, replica_groups=mesh['x'=4,'z'=16,'y'=4,'c'=2] {'x','z'}, dimensions={0} | all-to-all | bytes 262144 | tf_op jit(solution)/shard_map/all_to_all | solution.py:161
  56.0 0.7 shard_map.48
  56.8 5.5 %all-to-all-start.2 = ((bf16[64,8,128]{2,1,0:T(8,128)(2,1)}), bf16[64,8,128]{2,1,0:T(8,128)(2,1)S(1)}, u32[]{:S(2)}, u32[]{:S(2)}) async-start(bf16[64,8,128]{2,1,0:T(8,128)(2,1)} %shard_map.48), calls=%async_computation.2 | async-start | bytes 262144 | tf_op jit(solution)/shard_map/all_to_all | solution.py:165
  62.2 0.0 copy-done.1
  62.2 0.0 copy-done.3
  62.2 0.0 copy-done.4
  62.3 2.6 %shard_map.46.i_ref = f32[512,512]{1,0:T(8,128)S(1)} custom-call(bf16[512,512]{1,0:T(8,128)(2,1)S(1)} %copy-done.4, bf16[512,512]{1,0:T(8,128)(2,1)S(1)} %copy-done.1, bf16[512,512]{1,0:T(8,128)(2,1)S(1)} %copy-done.3), custom_call_target="tpu_custom_call" | custom-call | flops 536870912 | bytes 2621440 | tf_op jit(solution)/shard_map/pallas_call | solution.py:150
  64.8 11.5 %all-to-all-done.2 = bf16[64,8,128]{2,1,0:T(8,128)(2,1)S(1)} async-done(((bf16[64,8,128]{2,1,0:T(8,128)(2,1)}), bf16[64,8,128]{2,1,0:T(8,128)(2,1)S(1)}, u32[]{:S(2)}, u32[]{:S(2)}) %all-to-all-start.2) | async-done | bytes 131104 | tf_op jit(solution)/shard_map/all_to_all | solution.py:165
  76.4 1.8 %shard_map.49 = bf16[4,512,512]{2,1,0:T(8,128)(2,1)S(1)} custom-call(bf16[512,512]{1,0:T(8,128)(2,1)S(1)} %copy-done.4, f32[512,512]{1,0:T(8,128)S(1)} %shard_map.46.i_ref, bf16[512,128]{1,0:T(8,128)(2,1)S(1)} %bitcast.6), custom_call_target="tpu_custom_call" | custom-call | tf_op jit(solution)/shard_map/pallas_call | solution.py:166
  78.2 23.1 %all_to_all.22.own_ref = bf16[4,512,512]{2,1,0:T(8,128)(2,1)S(1)} all-to-all(bf16[4,512,512]{2,1,0:T(8,128)(2,1)S(1)} %shard_map.49), channel_id=1, replica_groups=mesh['x'=4,'z'=16,'y'=4,'c'=2] {'y'}, dimensions={0} | all-to-all | bytes 4194304 | tf_op jit(solution)/shard_map/all_to_all | solution.py:174
  101.3 9.4 %collective-permute-start.1 = (bf16[4,512,512]{2,1,0:T(8,128)(2,1)S(1)}, bf16[4,512,512]{2,1,0:T(8,128)(2,1)}, u32[]{:S(2)}, u32[]{:S(2)}) collective-permute-start(bf16[4,512,512]{2,1,0:T(8,128)(2,1)S(1)} %all_to_all.22.own_ref), channel_id=1, source_target_pairs={{0,1},{1,0},{2,3},{3,2},{4,5},{5,4},{6,7},{7,6},{8,9},{9,8},{10,11... | collective-permute-start | bytes 6291464 | tf_op jit(solution)/shard_map/ppermute | solution.py:175
  110.7 3.9 %collective-permute-done.1.far_ref = bf16[4,512,512]{2,1,0:T(8,128)(2,1)} collective-permute-done((bf16[4,512,512]{2,1,0:T(8,128)(2,1)S(1)}, bf16[4,512,512]{2,1,0:T(8,128)(2,1)}, u32[]{:S(2)}, u32[]{:S(2)}) %collective-permute-start.1) | collective-permute-done | bytes 2097184 | tf_op jit(solution)/shard_map/ppermute | solution.py:175
  114.6 0.9 all-gather.3.cloned.1.call-done
  115.5 4.6 %shard_map.50 = bf16[512,512]{1,0:T(8,128)(2,1)} custom-call(s32[1]{0:T(128)} %bitcast.core_ref, bf16[4,512,512]{2,1,0:T(8,128)(2,1)S(1)} %all_to_all.22.own_ref, bf16[4,512,512]{2,1,0:T(8,128)(2,1)} %collective-permute-done.1.far_ref, bf16[16,2,4,64,512]{4,3,2,1,0:T(8,128)(2,1)} %bitcast.7), custom_call_target="tpu_custom_call" | custom-call | tf_op jit(solution)/shard_map/pallas_call | solution.py:111
  (1 shorter events, 0.0 us)
Async XLA Ops:
  6.5 109.0 %all-gather.3.cloned.1.call-start = ((), (), s32[]{:S(2)}) async-start(), calls=%async_computation.4 | async-start | bytes 8650752 | tf_op jit(solution)/shard_map/all_gather | solution.py:149
  6.5 8.7 %collective-permute-start = (bf16[64,512]{1,0:T(8,128)(2,1)}, bf16[64,512]{1,0:T(8,128)(2,1)S(1)}, u32[]{:S(2)}, u32[]{:S(2)}) collective-permute-start(bf16[64,512]{1,0:T(8,128)(2,1)} %bitcast.8), channel_id=1, source_target_pairs={{0,256},{2,384},{4,0},{6,128},{128,258},{130,386},{132,2},{134,130... | collective-permute-start | bytes 196616 | tf_op jit(solution)/shard_map/ppermute | solution.py:134
  12.0 1.0 copy-start
  13.1 1.0 copy-start.2
  14.1 48.1 %copy-start.1 = (bf16[512,512]{1,0:T(8,128)(2,1)S(1)}, bf16[512,512]{1,0:T(8,128)(2,1)}, u32[]{:S(2)}) copy-start(bf16[512,512]{1,0:T(8,128)(2,1)} %k_ref.3) | copy-start | bytes 1572868
  14.1 48.1 %copy-start.3 = (bf16[512,512]{1,0:T(8,128)(2,1)S(1)}, bf16[512,512]{1,0:T(8,128)(2,1)}, u32[]{:S(2)}) copy-start(bf16[512,512]{1,0:T(8,128)(2,1)} %v_ref.3) | copy-start | bytes 1572868
  14.1 48.1 %copy-start.4 = (bf16[512,512]{1,0:T(8,128)(2,1)S(1)}, bf16[512,512]{1,0:T(8,128)(2,1)}, u32[]{:S(2)}) copy-start(bf16[512,512]{1,0:T(8,128)(2,1)} %q_ref.3) | copy-start | bytes 1572868
  56.8 19.6 %all-to-all-start.2 = ((bf16[64,8,128]{2,1,0:T(8,128)(2,1)}), bf16[64,8,128]{2,1,0:T(8,128)(2,1)S(1)}, u32[]{:S(2)}, u32[]{:S(2)}) async-start(bf16[64,8,128]{2,1,0:T(8,128)(2,1)} %shard_map.48), calls=%async_computation.2 | async-start | bytes 262144 | tf_op jit(solution)/shard_map/all_to_all | solution.py:165
  101.3 13.3 %collective-permute-start.1 = (bf16[4,512,512]{2,1,0:T(8,128)(2,1)S(1)}, bf16[4,512,512]{2,1,0:T(8,128)(2,1)}, u32[]{:S(2)}, u32[]{:S(2)}) collective-permute-start(bf16[4,512,512]{2,1,0:T(8,128)(2,1)S(1)} %all_to_all.22.own_ref), channel_id=1, source_target_pairs={{0,1},{1,0},{2,3},{3,2},{4,5},{5,4},{6,7},{7,6},{8,9},{9,8},{10,11... | collective-permute-start | bytes 6291464 | tf_op jit(solution)/shard_map/ppermute | solution.py:175
Sparse Core Ops, SparseCore 0:
  25.9 89.5 all-gather.2

commit v8 on v6

--- a/solution.py
+++ b/solution.py
@@ -30,29 +30,33 @@
         total = total + s_ref[c].astype(F32)
 
 
-def attention_kernel(q_ref, k_ref, v_ref, p_ref, o_ref):
+def intra_kernel(q_ref, k_ref, v_ref, o_ref):
     rows = q_ref.shape[0]
     blk = 256
     t = lax.broadcasted_iota(jnp.int32, (blk, blk), 0)
     s = lax.broadcasted_iota(jnp.int32, (blk, blk), 1)
     causal = t >= s
-    prefix = p_ref[...]
     for i in range(rows // blk):
         here = slice(i * blk, (i + 1) * blk)
-        q = q_ref[here, :]
-        attn = jnp.dot(q, prefix, preferred_element_type=F32)
+        attn = None
         for j in range(i + 1):
             there = slice(j * blk, (j + 1) * blk)
             scores = lax.dot_general(
-                q, k_ref[there, :], (((1,), (1,)), ((), ())), preferred_element_type=F32
+                q_ref[here, :], k_ref[there, :], (((1,), (1,)), ((), ())), preferred_element_type=F32
             )
             if i == j:
                 scores = jnp.where(causal, scores, 0.0)
-            attn += jnp.dot(scores.astype(BF), v_ref[there, :], preferred_element_type=F32)
-        scale = lax.rsqrt(jnp.mean(attn * attn, axis=-1, keepdims=True) + 1e-06)
-        hidden = (attn * scale).astype(BF)
-        for n in range(o_ref.shape[0]):
-            o_ref[n, here, :] = hidden
+            part = jnp.dot(scores.astype(BF), v_ref[there, :], preferred_element_type=F32)
+            attn = part if attn is None else attn + part
+        o_ref[here, :] = attn
+
+
+def attention_kernel(q_ref, i_ref, p_ref, o_ref):
+    attn = i_ref[...] + jnp.dot(q_ref[...], p_ref[...], preferred_element_type=F32)
+    scale = lax.rsqrt(jnp.mean(attn * attn, axis=-1, keepdims=True) + 1e-06)
+    hidden = (attn * scale).astype(BF)
+    for n in range(o_ref.shape[0]):
+        o_ref[n] = hidden
 
 
 def projection_kernel(core_ref, own_ref, far_ref, w_ref, o_ref, *scratch):
@@ -135,6 +139,16 @@
     w4 = lax.all_to_all(jnp.broadcast_to(w[None], (NX,) + w.shape), "x", 0, 0)
     states, w4 = lax.optimization_barrier((states, w4))
     w_all = lax.all_gather(w4, ("z", "c")).reshape((NZ, NC) + w4.shape)
+    intra = pl.pallas_call(
+        intra_kernel,
+        grid=(heads,),
+        out_shape=jax.ShapeDtypeStruct((rows, width), F32),
+        in_specs=[by_head] * 3, out_specs=by_head,
+        cost_estimate=pl.CostEstimate(
+            flops=4 * rows * rows * width, bytes_accessed=10 * rows * width, transcendentals=0
+        ),
+        compiler_params=params(),
+    )(queries, keys, values)
     part = width // N_CTX
     mine = lax.all_to_all(states.reshape(N_CTX, part, HEAD_DIM), ("x", "z"), 0, 0)
     scanned = pl.pallas_call(
@@ -145,10 +159,10 @@
         attention_kernel,
         grid=(heads,),
         out_shape=jax.ShapeDtypeStruct((NY, rows, width), BF),
-        in_specs=[by_head, by_head, by_head, state],
+        in_specs=[by_head, by_head, state],
         out_specs=pl.BlockSpec((NY, rows, HEAD_DIM), lambda h: (0, 0, h)),
         compiler_params=params(),
-    )(queries, keys, values, prefix)
+    )(queries, intra, prefix)
     hidden = lax.all_to_all(hidden, "y", 0, 0)
     other = lax.ppermute(hidden, "c", [(0, 1), (1, 0)])
     return project(me_c.astype(jnp.int32).reshape(1), hidden, other, w_all)

time: 128 us -> 127 us (level)
  blocking collectives: 83.8 us -> 63.8 us
  waiting for transfers between devices: 4.23 us -> 16.4 us
  starting transfers between devices: 14.1 us -> 20.3 us
  Pallas kernels: 9.44 us -> 11 us
    all_to_all x1 -> x0, blocking collectives: 19.7 us -> none  [local(): prefix = lax.all_to_all(scanned, ('x', 'z'), 0, 0).reshape(width, HEAD_DIM)]
    all_to_all x0 -> x1, waiting for transfers between devices: none -> 11.5 us  [local(): prefix = lax.all_to_all(scanned, ('x', 'z'), 0, 0).reshape(width, HEAD_DIM)]
    all_to_all x0 -> x1, starting transfers between devices: none -> 5.46 us  [local(): prefix = lax.all_to_all(scanned, ('x', 'z'), 0, 0).reshape(width, HEAD_DIM)]
    pallas_call x0 -> x1, Pallas kernels: none -> 2.58 us  [local(): pl.pallas_call(intra_kernel, grid=(heads,), out_shape=jax.ShapeDtypeStruc...]
    pallas_call x1, Pallas kernels: 3.52 us -> 1.81 us  [local(): pl.pallas_call(attention_kernel, grid=(heads,), out_shape=jax.ShapeDtypeS...]
  transfers between devices with their start and end apart: 3 -> 4, of which waited for: 2 -> 3; matrix products, arithmetic and copies ran while one was open for 0% -> 0% of each run, Pallas kernels for 4% -> 5%
where the time goes in v8:
time: 127 us
  blocking collectives  63.8 us (50%)
  starting transfers between devices  20.3 us (16%)
  waiting for transfers between devices  16.4 us (13%)
  between operations  13.5 us (11%)
  Pallas kernels  11 us (9%)
  local copies, waits for them, and re-layouts  2.11 us (2%)
    all_to_all x1, blocking collectives, local(): lax.all_to_all(states.reshape(N_CTX, part, HEAD_DIM), ('x', 'z'), 0, 0)  30.2 us
    all_to_all x1, blocking collectives, local(): hidden = lax.all_to_all(hidden, 'y', 0, 0)  23.1 us
    all_to_all x1, waiting for transfers between devices, local(): prefix = lax.all_to_all(scanned, ('x', 'z'), 0, 0).reshape(width, HEAD_DIM)  11.5 us
    all_to_all x1, blocking collectives, local(): w4 = lax.all_to_all(jnp.broadcast_to(w[None], (NX,) + w.shape), 'x', 0, 0)  10.4 us
    ppermute x1, starting transfers between devices, local(): other = lax.ppermute(hidden, 'c', [(0, 1), (1, 0)])  9.39 us
    ppermute x1, starting transfers between devices, local(): lax.ppermute(out_weight.T, ('x', 'y'), [(x * NY + y, (y + HOME) % NX * NY...  5.47 us
    all_to_all x1, starting transfers between devices, local(): prefix = lax.all_to_all(scanned, ('x', 'z'), 0, 0).reshape(width, HEAD_DIM)  5.46 us
    pallas_call x1, Pallas kernels, project(): pl.pallas_call(projection_kernel, in_specs=[pl.BlockSpec(memory_space=plt...  4.68 us
  transfers between devices with their start and end apart: 4, of which 3 were waited for; matrix products, arithmetic and copies ran while one was open for 0% of the time, Pallas kernels for 5%

profile of v8, /device:TPU:1, one launch (start us, length us, event | category | flops | bytes accessed | tf_op | source)
XLA Modules:
  0.0 127.1 jit_solution(10207088494797220940)
XLA Ops:
  6.5 0.0 all-gather.3.cloned.1.call-start
  6.5 5.5 %collective-permute-start = (bf16[64,512]{1,0:T(8,128)(2,1)}, bf16[64,512]{1,0:T(8,128)(2,1)S(1)}, u32[]{:S(2)}, u32[]{:S(2)}) collective-permute-start(bf16[64,512]{1,0:T(8,128)(2,1)} %bitcast.8), channel_id=1, source_target_pairs={{0,256},{2,384},{4,0},{6,128},{128,258},{130,386},{132,2},{134,130... | collective-permute-start | bytes 196616 | tf_op jit(solution)/shard_map/ppermute | solution.py:126
  12.0 0.0 copy-start
  12.0 1.0 copy-done
  13.1 0.0 copy-start.2
  13.1 1.0 copy-done.2
  14.1 0.0 copy-start.1
  14.1 0.0 copy-start.3
  14.1 0.0 copy-start.4
  14.1 1.2 shard_map.47
  15.3 0.0 collective-permute-done
  15.3 10.4 %all_to_all.20 = bf16[4,64,512]{2,1,0:T(8,128)(2,1)} all-to-all(bf16[4,64,512]{2,1,0:T(8,128)(2,1)S(1)} %broadcast_in_dim.2), channel_id=1, replica_groups=mesh['x'=4,'z'=16,'y'=4,'c'=2] {'x'}, dimensions={0} | all-to-all | bytes 524288 | tf_op jit(solution)/shard_map/all_to_all | solution.py:139
  25.8 0.0 all-gather.3.cloned.1.call-update
  25.8 30.2 %all_to_all.21.s_ref = bf16[64,8,128]{2,1,0:T(8,128)(2,1)S(1)} all-to-all(bf16[64,8,128]{2,1,0:T(8,128)(2,1)S(1)} %bitcast.5), channel_id=1, replica_groups=mesh['x'=4,'z'=16,'y'=4,'c'=2] {'x','z'}, dimensions={0} | all-to-all | bytes 262144 | tf_op jit(solution)/shard_map/all_to_all | solution.py:153
  56.0 0.7 shard_map.48
  56.8 5.5 %all-to-all-start.2 = ((bf16[64,8,128]{2,1,0:T(8,128)(2,1)}), bf16[64,8,128]{2,1,0:T(8,128)(2,1)S(1)}, u32[]{:S(2)}, u32[]{:S(2)}) async-start(bf16[64,8,128]{2,1,0:T(8,128)(2,1)} %shard_map.48), calls=%async_computation.2 | async-start | bytes 262144 | tf_op jit(solution)/shard_map/all_to_all | solution.py:157
  62.2 0.0 copy-done.1
  62.2 0.0 copy-done.3
  62.2 0.0 copy-done.4
  62.3 2.6 %shard_map.46.i_ref = f32[512,512]{1,0:T(8,128)S(1)} custom-call(bf16[512,512]{1,0:T(8,128)(2,1)S(1)} %copy-done.4, bf16[512,512]{1,0:T(8,128)(2,1)S(1)} %copy-done.1, bf16[512,512]{1,0:T(8,128)(2,1)S(1)} %copy-done.3), custom_call_target="tpu_custom_call" | custom-call | flops 536870912 | bytes 2621440 | tf_op jit(solution)/shard_map/pallas_call | solution.py:142
  64.8 11.5 %all-to-all-done.2 = bf16[64,8,128]{2,1,0:T(8,128)(2,1)S(1)} async-done(((bf16[64,8,128]{2,1,0:T(8,128)(2,1)}), bf16[64,8,128]{2,1,0:T(8,128)(2,1)S(1)}, u32[]{:S(2)}, u32[]{:S(2)}) %all-to-all-start.2) | async-done | bytes 131104 | tf_op jit(solution)/shard_map/all_to_all | solution.py:157
  76.4 1.8 %shard_map.49 = bf16[4,512,512]{2,1,0:T(8,128)(2,1)S(1)} custom-call(bf16[512,512]{1,0:T(8,128)(2,1)S(1)} %copy-done.4, f32[512,512]{1,0:T(8,128)S(1)} %shard_map.46.i_ref, bf16[512,128]{1,0:T(8,128)(2,1)S(1)} %bitcast.6), custom_call_target="tpu_custom_call" | custom-call | tf_op jit(solution)/shard_map/pallas_call | solution.py:158
  78.2 23.1 %all_to_all.22.own_ref = bf16[4,512,512]{2,1,0:T(8,128)(2,1)S(1)} all-to-all(bf16[4,512,512]{2,1,0:T(8,128)(2,1)S(1)} %shard_map.49), channel_id=1, replica_groups=mesh['x'=4,'z'=16,'y'=4,'c'=2] {'y'}, dimensions={0} | all-to-all | bytes 4194304 | tf_op jit(solution)/shard_map/all_to_all | solution.py:166
  101.3 9.4 %collective-permute-start.1 = (bf16[4,512,512]{2,1,0:T(8,128)(2,1)S(1)}, bf16[4,512,512]{2,1,0:T(8,128)(2,1)}, u32[]{:S(2)}, u32[]{:S(2)}) collective-permute-start(bf16[4,512,512]{2,1,0:T(8,128)(2,1)S(1)} %all_to_all.22.own_ref), channel_id=1, source_target_pairs={{0,1},{1,0},{2,3},{3,2},{4,5},{5,4},{6,7},{7,6},{8,9},{9,8},{10,11... | collective-permute-start | bytes 6291464 | tf_op jit(solution)/shard_map/ppermute | solution.py:167
  110.7 3.9 %collective-permute-done.1.far_ref = bf16[4,512,512]{2,1,0:T(8,128)(2,1)} collective-permute-done((bf16[4,512,512]{2,1,0:T(8,128)(2,1)S(1)}, bf16[4,512,512]{2,1,0:T(8,128)(2,1)}, u32[]{:S(2)}, u32[]{:S(2)}) %collective-permute-start.1) | collective-permute-done | bytes 2097184 | tf_op jit(solution)/shard_map/ppermute | solution.py:167
  114.6 0.9 all-gather.3.cloned.1.call-done
  115.5 4.7 %shard_map.50 = bf16[512,512]{1,0:T(8,128)(2,1)} custom-call(s32[1]{0:T(128)} %bitcast.core_ref, bf16[4,512,512]{2,1,0:T(8,128)(2,1)S(1)} %all_to_all.22.own_ref, bf16[4,512,512]{2,1,0:T(8,128)(2,1)} %collective-permute-done.1.far_ref, bf16[16,2,4,64,512]{4,3,2,1,0:T(8,128)(2,1)} %bitcast.7), custom_call_target="tpu_custom_call" | custom-call | tf_op jit(solution)/shard_map/pallas_call | solution.py:104
  (1 shorter events, 0.0 us)
Async XLA Ops:
  6.5 109.0 %all-gather.3.cloned.1.call-start = ((), (), s32[]{:S(2)}) async-start(), calls=%async_computation.4 | async-start | bytes 8650752 | tf_op jit(solution)/shard_map/all_gather | solution.py:141
  6.5 8.7 %collective-permute-start = (bf16[64,512]{1,0:T(8,128)(2,1)}, bf16[64,512]{1,0:T(8,128)(2,1)S(1)}, u32[]{:S(2)}, u32[]{:S(2)}) collective-permute-start(bf16[64,512]{1,0:T(8,128)(2,1)} %bitcast.8), channel_id=1, source_target_pairs={{0,256},{2,384},{4,0},{6,128},{128,258},{130,386},{132,2},{134,130... | collective-permute-start | bytes 196616 | tf_op jit(solution)/shard_map/ppermute | solution.py:126
  12.0 1.0 copy-start
  13.1 1.0 copy-start.2
  14.1 48.1 %copy-start.1 = (bf16[512,512]{1,0:T(8,128)(2,1)S(1)}, bf16[512,512]{1,0:T(8,128)(2,1)}, u32[]{:S(2)}) copy-start(bf16[512,512]{1,0:T(8,128)(2,1)} %k_ref.3) | copy-start | bytes 1572868
  14.1 48.1 %copy-start.3 = (bf16[512,512]{1,0:T(8,128)(2,1)S(1)}, bf16[512,512]{1,0:T(8,128)(2,1)}, u32[]{:S(2)}) copy-start(bf16[512,512]{1,0:T(8,128)(2,1)} %v_ref.3) | copy-start | bytes 1572868
  14.1 48.1 %copy-start.4 = (bf16[512,512]{1,0:T(8,128)(2,1)S(1)}, bf16[512,512]{1,0:T(8,128)(2,1)}, u32[]{:S(2)}) copy-start(bf16[512,512]{1,0:T(8,128)(2,1)} %q_ref.3) | copy-start | bytes 1572868
  56.8 19.6 %all-to-all-start.2 = ((bf16[64,8,128]{2,1,0:T(8,128)(2,1)}), bf16[64,8,128]{2,1,0:T(8,128)(2,1)S(1)}, u32[]{:S(2)}, u32[]{:S(2)}) async-start(bf16[64,8,128]{2,1,0:T(8,128)(2,1)} %shard_map.48), calls=%async_computation.2 | async-start | bytes 262144 | tf_op jit(solution)/shard_map/all_to_all | solution.py:157
  101.3 13.3 %collective-permute-start.1 = (bf16[4,512,512]{2,1,0:T(8,128)(2,1)S(1)}, bf16[4,512,512]{2,1,0:T(8,128)(2,1)}, u32[]{:S(2)}, u32[]{:S(2)}) collective-permute-start(bf16[4,512,512]{2,1,0:T(8,128)(2,1)S(1)} %all_to_all.22.own_ref), channel_id=1, source_target_pairs={{0,1},{1,0},{2,3},{3,2},{4,5},{5,4},{6,7},{7,6},{8,9},{9,8},{10,11... | collective-permute-start | bytes 6291464 | tf_op jit(solution)/shard_map/ppermute | solution.py:167
Sparse Core Ops, SparseCore 0:
  25.9 89.5 all-gather.2

commit v9 on v7

--- a/solution.py
+++ b/solution.py
@@ -30,33 +30,29 @@
         total = total + s_ref[c].astype(F32)
 
 
-def intra_kernel(q_ref, k_ref, v_ref, o_ref):
+def attention_kernel(q_ref, k_ref, v_ref, p_ref, o_ref):
     rows = q_ref.shape[0]
     blk = 256
     t = lax.broadcasted_iota(jnp.int32, (blk, blk), 0)
     s = lax.broadcasted_iota(jnp.int32, (blk, blk), 1)
     causal = t >= s
+    prefix = p_ref[...]
     for i in range(rows // blk):
         here = slice(i * blk, (i + 1) * blk)
-        attn = None
+        q = q_ref[here, :]
+        attn = jnp.dot(q, prefix, preferred_element_type=F32)
         for j in range(i + 1):
             there = slice(j * blk, (j + 1) * blk)
             scores = lax.dot_general(
-                q_ref[here, :], k_ref[there, :], (((1,), (1,)), ((), ())), preferred_element_type=F32
+                q, k_ref[there, :], (((1,), (1,)), ((), ())), preferred_element_type=F32
             )
             if i == j:
                 scores = jnp.where(causal, scores, 0.0)
-            part = jnp.dot(scores.astype(BF), v_ref[there, :], preferred_element_type=F32)
-            attn = part if attn is None else attn + part
-        o_ref[here, :] = attn
-
-
-def attention_kernel(q_ref, i_ref, p_ref, o_ref):
-    attn = i_ref[...] + jnp.dot(q_ref[...], p_ref[...], preferred_element_type=F32)
-    scale = lax.rsqrt(jnp.mean(attn * attn, axis=-1, keepdims=True) + 1e-06)
-    hidden = (attn * scale).astype(BF)
-    for n in range(o_ref.shape[0]):
-        o_ref[n] = hidden
+            attn += jnp.dot(scores.astype(BF), v_ref[there, :], preferred_element_type=F32)
+        scale = lax.rsqrt(jnp.mean(attn * attn, axis=-1, keepdims=True) + 1e-06)
+        hidden = (attn * scale).astype(BF)
+        for n in range(o_ref.shape[0]):
+            o_ref[n, here, :] = hidden
 
 
 def projection_kernel(core_ref, own_ref, far_ref, w_ref, o_ref, *scratch):
@@ -147,16 +143,6 @@
     w4 = lax.all_to_all(jnp.broadcast_to(w[None], (NX,) + w.shape), "x", 0, 0)
     states, w4 = lax.optimization_barrier((states, w4))
     w_all = lax.all_gather(w4, ("z", "c")).reshape((NZ, NC) + w4.shape)
-    intra = pl.pallas_call(
-        intra_kernel,
-        grid=(heads,),
-        out_shape=jax.ShapeDtypeStruct((rows, width), F32),
-        in_specs=[by_head] * 3, out_specs=by_head,
-        cost_estimate=pl.CostEstimate(
-            flops=4 * rows * rows * width, bytes_accessed=10 * rows * width, transcendentals=0
-        ),
-        compiler_params=params(),
-    )(queries, keys, values)
     part = width // N_CTX
     mine = lax.all_to_all(states.reshape(N_CTX, part, HEAD_DIM), ("x", "z"), 0, 0)
     scanned = pl.pallas_call(
@@ -167,10 +153,10 @@
         attention_kernel,
         grid=(heads,),
         out_shape=jax.ShapeDtypeStruct((NY, rows, width), BF),
-        in_specs=[by_head, by_head, state],
+        in_specs=[by_head, by_head, by_head, state],
         out_specs=pl.BlockSpec((NY, rows, HEAD_DIM), lambda h: (0, 0, h)),
         compiler_params=params(),
-    )(queries, intra, prefix)
+    )(queries, keys, values, prefix)
     hidden = lax.all_to_all(hidden, "y", 0, 0)
     other = lax.ppermute(hidden, "c", [(0, 1), (1, 0)])
     return project(me_c.astype(jnp.int32).reshape(1), hidden, other, w_all)

time: 127 us -> 128 us (level)
  blocking collectives: 63.8 us -> 83.8 us
  waiting for transfers between devices: 16.4 us -> 4.23 us
  starting transfers between devices: 20.3 us -> 14.1 us
  Pallas kernels: 10.9 us -> 9.36 us
    all_to_all x0 -> x1, blocking collectives: none -> 19.7 us  [local(): prefix = lax.all_to_all(scanned, ('x', 'z'), 0, 0).reshape(width, HEAD_DIM)]
    all_to_all x1 -> x0, waiting for transfers between devices: 11.5 us -> none  [local(): prefix = lax.all_to_all(scanned, ('x', 'z'), 0, 0).reshape(width, HEAD_DIM)]
    all_to_all x1 -> x0, starting transfers between devices: 5.46 us -> none  [local(): prefix = lax.all_to_all(scanned, ('x', 'z'), 0, 0).reshape(width, HEAD_DIM)]
    pallas_call x1 -> x0, Pallas kernels: 2.58 us -> none  [local(): pl.pallas_call(intra_kernel, grid=(heads,), out_shape=jax.ShapeDtypeStruc...]
    pallas_call x1, Pallas kernels: 1.81 us -> 3.52 us  [local(): pl.pallas_call(attention_kernel, grid=(heads,), out_shape=jax.ShapeDtypeS...]
  transfers between devices with their start and end apart: 4 -> 3, of which waited for: 3 -> 2; matrix products, arithmetic and copies ran while one was open for 0% -> 0% of each run, Pallas kernels for 5% -> 4%
where the time goes in v9:
time: 128 us; the launch traced here: 127 us
  blocking collectives  83.8 us (65%)
  starting transfers between devices  14.1 us (11%)
  between operations  13.5 us (11%)
  Pallas kernels  9.36 us (7%)
  waiting for transfers between devices  4.23 us (3%)
  local copies, waits for them, and re-layouts  2.11 us (2%)
    all_to_all x1, blocking collectives, local(): lax.all_to_all(states.reshape(N_CTX, part, HEAD_DIM), ('x', 'z'), 0, 0)  30.2 us
    all_to_all x1, blocking collectives, local(): hidden = lax.all_to_all(hidden, 'y', 0, 0)  23.5 us
    all_to_all x1, blocking collectives, local(): prefix = lax.all_to_all(scanned, ('x', 'z'), 0, 0).reshape(width, HEAD_DIM)  19.7 us
    all_to_all x1, blocking collectives, local(): w4 = lax.all_to_all(jnp.broadcast_to(w[None], (NX,) + w.shape), 'x', 0, 0)  10.4 us
    ppermute x1, starting transfers between devices, local(): other = lax.ppermute(hidden, 'c', [(0, 1), (1, 0)])  8.65 us
    ppermute x1, starting transfers between devices, local(): lax.ppermute(out_weight.T, ('x', 'y'), [(x * NY + y, (y + HOME) % NX * NY...  5.47 us
    pallas_call x1, Pallas kernels, project(): pl.pallas_call(projection_kernel, in_specs=[pl.BlockSpec(memory_space=plt...  4.61 us
    ppermute x1, waiting for transfers between devices, local(): other = lax.ppermute(hidden, 'c', [(0, 1), (1, 0)])  3.89 us
  transfers between devices with their start and end apart: 3, of which 2 were waited for; matrix products, arithmetic and copies ran while one was open for 0% of the time, Pallas kernels for 4%

profile of v9, /device:TPU:1, one launch (start us, length us, event | category | flops | bytes accessed | tf_op | source)
XLA Modules:
  0.0 127.2 jit_solution(9657495462488894153)
XLA Ops:
  6.5 0.0 all-gather.3.cloned.1.call-start
  6.5 5.5 %collective-permute-start = (bf16[64,512]{1,0:T(8,128)(2,1)}, bf16[64,512]{1,0:T(8,128)(2,1)S(1)}, u32[]{:S(2)}, u32[]{:S(2)}) collective-permute-start(bf16[64,512]{1,0:T(8,128)(2,1)} %bitcast.8), channel_id=1, source_target_pairs={{0,256},{2,384},{4,0},{6,128},{128,258},{130,386},{132,2},{134,130... | collective-permute-start | bytes 196616 | tf_op jit(solution)/shard_map/ppermute | solution.py:130
  12.0 0.0 copy-start
  12.0 1.0 copy-done
  13.1 0.0 copy-start.2
  13.1 1.0 copy-done.2
  14.1 0.0 copy-start.1
  14.1 0.0 copy-start.3
  14.1 0.0 copy-start.4
  14.1 1.2 shard_map.46
  15.3 0.0 collective-permute-done
  15.3 10.4 %all_to_all.20 = bf16[4,64,512]{2,1,0:T(8,128)(2,1)} all-to-all(bf16[4,64,512]{2,1,0:T(8,128)(2,1)S(1)} %broadcast_in_dim.2), channel_id=1, replica_groups=mesh['x'=4,'z'=16,'y'=4,'c'=2] {'x'}, dimensions={0} | all-to-all | bytes 524288 | tf_op jit(solution)/shard_map/all_to_all | solution.py:143
  25.8 0.0 all-gather.3.cloned.1.call-update
  25.8 30.2 %all_to_all.21.s_ref = bf16[64,8,128]{2,1,0:T(8,128)(2,1)S(1)} all-to-all(bf16[64,8,128]{2,1,0:T(8,128)(2,1)S(1)} %bitcast.5), channel_id=1, replica_groups=mesh['x'=4,'z'=16,'y'=4,'c'=2] {'x','z'}, dimensions={0} | all-to-all | bytes 262144 | tf_op jit(solution)/shard_map/all_to_all | solution.py:147
  56.0 0.1 shard_map.47
  56.1 19.7 %all_to_all.22 = bf16[64,8,128]{2,1,0:T(8,128)(2,1)S(1)} all-to-all(bf16[64,8,128]{2,1,0:T(8,128)(2,1)S(1)} %shard_map.47), channel_id=1, replica_groups=mesh['x'=4,'z'=16,'y'=4,'c'=2] {'x','z'}, dimensions={0} | all-to-all | bytes 262144 | tf_op jit(solution)/shard_map/all_to_all | solution.py:151
  75.8 0.0 copy-done.1
  75.8 0.0 copy-done.3
  75.8 0.0 copy-done.4
  75.8 3.5 %shard_map.48 = bf16[4,512,512]{2,1,0:T(8,128)(2,1)S(1)} custom-call(bf16[512,512]{1,0:T(8,128)(2,1)S(1)} %copy-done.4, bf16[512,512]{1,0:T(8,128)(2,1)S(1)} %copy-done.1, bf16[512,512]{1,0:T(8,128)(2,1)S(1)} %copy-done.3, bf16[512,128]{1,0:T(8,128)(2,1)S(1)} %bitcast.6), custom_call_target="tpu_custom_call" | custom-call | tf_op jit(solution)/shard_map/pallas_call | solution.py:152
  79.3 23.5 %all_to_all.23.own_ref = bf16[4,512,512]{2,1,0:T(8,128)(2,1)S(1)} all-to-all(bf16[4,512,512]{2,1,0:T(8,128)(2,1)S(1)} %shard_map.48), channel_id=1, replica_groups=mesh['x'=4,'z'=16,'y'=4,'c'=2] {'y'}, dimensions={0} | all-to-all | bytes 4194304 | tf_op jit(solution)/shard_map/all_to_all | solution.py:160
  102.8 8.7 %collective-permute-start.1 = (bf16[4,512,512]{2,1,0:T(8,128)(2,1)S(1)}, bf16[4,512,512]{2,1,0:T(8,128)(2,1)}, u32[]{:S(2)}, u32[]{:S(2)}) collective-permute-start(bf16[4,512,512]{2,1,0:T(8,128)(2,1)S(1)} %all_to_all.23.own_ref), channel_id=1, source_target_pairs={{0,1},{1,0},{2,3},{3,2},{4,5},{5,4},{6,7},{7,6},{8,9},{9,8},{10,11... | collective-permute-start | bytes 6291464 | tf_op jit(solution)/shard_map/ppermute | solution.py:161
  111.5 3.9 %collective-permute-done.1.far_ref = bf16[4,512,512]{2,1,0:T(8,128)(2,1)} collective-permute-done((bf16[4,512,512]{2,1,0:T(8,128)(2,1)S(1)}, bf16[4,512,512]{2,1,0:T(8,128)(2,1)}, u32[]{:S(2)}, u32[]{:S(2)}) %collective-permute-start.1) | collective-permute-done | bytes 2097184 | tf_op jit(solution)/shard_map/ppermute | solution.py:161
  115.4 0.3 all-gather.3.cloned.1.call-done
  115.7 4.6 %shard_map.49 = bf16[512,512]{1,0:T(8,128)(2,1)} custom-call(s32[1]{0:T(128)} %bitcast.core_ref, bf16[4,512,512]{2,1,0:T(8,128)(2,1)S(1)} %all_to_all.23.own_ref, bf16[4,512,512]{2,1,0:T(8,128)(2,1)} %collective-permute-done.1.far_ref, bf16[16,2,4,64,512]{4,3,2,1,0:T(8,128)(2,1)} %bitcast.7), custom_call_target="tpu_custom_call" | custom-call | tf_op jit(solution)/shard_map/pallas_call | solution.py:107
  (1 shorter events, 0.0 us)
Async XLA Ops:
  6.5 109.1 %all-gather.3.cloned.1.call-start = ((), (), s32[]{:S(2)}) async-start(), calls=%async_computation.4 | async-start | bytes 8650752 | tf_op jit(solution)/shard_map/all_gather | solution.py:145
  6.5 8.7 %collective-permute-start = (bf16[64,512]{1,0:T(8,128)(2,1)}, bf16[64,512]{1,0:T(8,128)(2,1)S(1)}, u32[]{:S(2)}, u32[]{:S(2)}) collective-permute-start(bf16[64,512]{1,0:T(8,128)(2,1)} %bitcast.8), channel_id=1, source_target_pairs={{0,256},{2,384},{4,0},{6,128},{128,258},{130,386},{132,2},{134,130... | collective-permute-start | bytes 196616 | tf_op jit(solution)/shard_map/ppermute | solution.py:130
  12.0 1.0 copy-start
  13.1 1.0 copy-start.2
  14.1 61.7 %copy-start.1 = (bf16[512,512]{1,0:T(8,128)(2,1)S(1)}, bf16[512,512]{1,0:T(8,128)(2,1)}, u32[]{:S(2)}) copy-start(bf16[512,512]{1,0:T(8,128)(2,1)} %k_ref.3) | copy-start | bytes 1572868
  14.1 61.7 %copy-start.3 = (bf16[512,512]{1,0:T(8,128)(2,1)S(1)}, bf16[512,512]{1,0:T(8,128)(2,1)}, u32[]{:S(2)}) copy-start(bf16[512,512]{1,0:T(8,128)(2,1)} %v_ref.3) | copy-start | bytes 1572868
  14.1 61.7 %copy-start.4 = (bf16[512,512]{1,0:T(8,128)(2,1)S(1)}, bf16[512,512]{1,0:T(8,128)(2,1)}, u32[]{:S(2)}) copy-start(bf16[512,512]{1,0:T(8,128)(2,1)} %q_ref.1) | copy-start | bytes 1572868
  102.8 12.6 %collective-permute-start.1 = (bf16[4,512,512]{2,1,0:T(8,128)(2,1)S(1)}, bf16[4,512,512]{2,1,0:T(8,128)(2,1)}, u32[]{:S(2)}, u32[]{:S(2)}) collective-permute-start(bf16[4,512,512]{2,1,0:T(8,128)(2,1)S(1)} %all_to_all.23.own_ref), channel_id=1, source_target_pairs={{0,1},{1,0},{2,3},{3,2},{4,5},{5,4},{6,7},{7,6},{8,9},{9,8},{10,11... | collective-permute-start | bytes 6291464 | tf_op jit(solution)/shard_map/ppermute | solution.py:161
Sparse Core Ops, SparseCore 0:
  25.9 89.7 all-gather.2

commit v10 on v9

--- a/solution.py
+++ b/solution.py
@@ -9,6 +9,7 @@
 NX, NZ, NY, NC = 4, 16, 4, 2
 N_CTX = NX * NZ
 HOME = 2
+PARTS = ((0, 0, 1), (0, 1, 3), (1, 0, 2), (1, 2, 2))
 BF = jnp.bfloat16
 F32 = jnp.float32
 
@@ -56,31 +57,27 @@
 
 
 def projection_kernel(core_ref, own_ref, far_ref, w_ref, o_ref, *scratch):
-    parts, (other_ref, acc_ref, out_ref, sem) = scratch[:4], scratch[4:]
+    parts, (other_ref, acc_ref, out_ref, sem) = scratch[:len(PARTS)], scratch[len(PARTS):]
     core = core_ref[0]
-    blocks, _, per, cols, depth = parts[0].shape
-    rows_of = [(k, first) for k in range(NC) for first in range(0, NY, per)]
+    blocks, _, _, cols, depth = parts[0].shape
     copies = [
         pltpu.make_async_copy(
             w_ref.at[pl.ds(core * blocks, blocks), pl.ds(core ^ k, 1), pl.ds(first, per)], part, sem.at[n]
         )
-        for n, ((k, first), part) in enumerate(zip(rows_of, parts))
+        for n, ((k, first, per), part) in enumerate(zip(PARTS, parts))
     ]
     other = pltpu.make_async_copy(far_ref, other_ref, sem.at[len(copies)])
     halves = (pl.ds(0, o_ref.shape[0] // 2), pl.ds(o_ref.shape[0] // 2, o_ref.shape[0] // 2))
-    outs = [pltpu.make_async_copy(out_ref.at[r], o_ref.at[r], sem.at[5 + n]) for n, r in enumerate(halves)]
-    copies[0].start()
-    copies[1].start()
-    other.start()
-    copies[2].start()
-    copies[3].start()
+    outs = [pltpu.make_async_copy(out_ref.at[r], o_ref.at[r], sem.at[len(copies) + 1 + n]) for n, r in enumerate(halves)]
+    for copy in copies[:2] + [other] + copies[2:]:
+        copy.start()
     half = own_ref.shape[1] // 2
-    for n, (k, first) in enumerate(rows_of):
+    for n, (k, first, per) in enumerate(PARTS):
         copies[n].wait()
-        if n == len(rows_of) // NC:
+        if n == 2:
             other.wait()
         h_ref = own_ref if k == 0 else other_ref
-        last = n == len(rows_of) - 1
+        last = n == len(PARTS) - 1
         for rows in (slice(0, half), slice(half, 2 * half)) if last else (slice(0, 2 * half),):
             total = None
             for i in range(per):
@@ -102,13 +99,13 @@
 def project(core, own, other, w_all):
     sources, rows, depth = own.shape
     cols = w_all.shape[3]
-    blocks, per = NZ // NC, NY // 2
+    blocks = NZ // NC
     anywhere, vmem = pl.BlockSpec(memory_space=pl.ANY), pl.BlockSpec(memory_space=pltpu.VMEM)
     return pl.pallas_call(
         projection_kernel,
         in_specs=[pl.BlockSpec(memory_space=pltpu.SMEM), vmem, anywhere, anywhere],
         out_specs=anywhere,
-        scratch_shapes=[pltpu.VMEM((blocks, 1, per, cols, depth), BF)] * 4 + [
+        scratch_shapes=[pltpu.VMEM((blocks, 1, per, cols, depth), BF) for _, _, per in PARTS] + [
             pltpu.VMEM((sources, rows, depth), BF),
             pltpu.VMEM((rows, blocks * cols), F32),
             pltpu.VMEM((rows, blocks * cols), BF),

time: 128 us -> 128 us (level)
  no operation moved by 1% of the time
where the time goes in v10:
time: 128 us; the launch traced here: 127 us
  blocking collectives  83.8 us (65%)
  starting transfers between devices  14.1 us (11%)
  between operations  13.5 us (11%)
  Pallas kernels  9.37 us (7%)
  waiting for transfers between devices  4.23 us (3%)
  local copies, waits for them, and re-layouts  2.11 us (2%)
    all_to_all x1, blocking collectives, local(): lax.all_to_all(states.reshape(N_CTX, part, HEAD_DIM), ('x', 'z'), 0, 0)  30.2 us
    all_to_all x1, blocking collectives, local(): hidden = lax.all_to_all(hidden, 'y', 0, 0)  23.5 us
    all_to_all x1, blocking collectives, local(): prefix = lax.all_to_all(scanned, ('x', 'z'), 0, 0).reshape(width, HEAD_DIM)  19.7 us
    all_to_all x1, blocking collectives, local(): w4 = lax.all_to_all(jnp.broadcast_to(w[None], (NX,) + w.shape), 'x', 0, 0)  10.4 us
    ppermute x1, starting transfers between devices, local(): other = lax.ppermute(hidden, 'c', [(0, 1), (1, 0)])  8.65 us
    ppermute x1, starting transfers between devices, local(): lax.ppermute(out_weight.T, ('x', 'y'), [(x * NY + y, (y + HOME) % NX * NY...  5.47 us
    pallas_call x1, Pallas kernels, project(): pl.pallas_call(projection_kernel, in_specs=[pl.BlockSpec(memory_space=plt...  4.62 us
    ppermute x1, waiting for transfers between devices, local(): other = lax.ppermute(hidden, 'c', [(0, 1), (1, 0)])  3.89 us
  transfers between devices with their start and end apart: 3, of which 2 were waited for; matrix products, arithmetic and copies ran while one was open for 0% of the time, Pallas kernels for 4%

profile of v10, /device:TPU:1, one launch (start us, length us, event | category | flops | bytes accessed | tf_op | source)
XLA Modules:
  0.0 127.2 jit_solution(13512029492277697322)
XLA Ops:
  6.5 0.0 all-gather.3.cloned.1.call-start
  6.5 5.5 %collective-permute-start = (bf16[64,512]{1,0:T(8,128)(2,1)}, bf16[64,512]{1,0:T(8,128)(2,1)S(1)}, u32[]{:S(2)}, u32[]{:S(2)}) collective-permute-start(bf16[64,512]{1,0:T(8,128)(2,1)} %bitcast.8), channel_id=1, source_target_pairs={{0,256},{2,384},{4,0},{6,128},{128,258},{130,386},{132,2},{134,130... | collective-permute-start | bytes 196616 | tf_op jit(solution)/shard_map/ppermute | solution.py:127
  12.0 0.0 copy-start
  12.0 1.0 copy-done
  13.1 0.0 copy-start.2
  13.1 1.0 copy-done.2
  14.1 0.0 copy-start.1
  14.1 0.0 copy-start.3
  14.1 0.0 copy-start.4
  14.1 1.2 shard_map.46
  15.3 0.0 collective-permute-done
  15.3 10.4 %all_to_all.20 = bf16[4,64,512]{2,1,0:T(8,128)(2,1)} all-to-all(bf16[4,64,512]{2,1,0:T(8,128)(2,1)S(1)} %broadcast_in_dim.2), channel_id=1, replica_groups=mesh['x'=4,'z'=16,'y'=4,'c'=2] {'x'}, dimensions={0} | all-to-all | bytes 524288 | tf_op jit(solution)/shard_map/all_to_all | solution.py:140
  25.8 0.0 all-gather.3.cloned.1.call-update
  25.8 30.2 %all_to_all.21.s_ref = bf16[64,8,128]{2,1,0:T(8,128)(2,1)S(1)} all-to-all(bf16[64,8,128]{2,1,0:T(8,128)(2,1)S(1)} %bitcast.5), channel_id=1, replica_groups=mesh['x'=4,'z'=16,'y'=4,'c'=2] {'x','z'}, dimensions={0} | all-to-all | bytes 262144 | tf_op jit(solution)/shard_map/all_to_all | solution.py:144
  56.0 0.1 shard_map.47
  56.1 19.7 %all_to_all.22 = bf16[64,8,128]{2,1,0:T(8,128)(2,1)S(1)} all-to-all(bf16[64,8,128]{2,1,0:T(8,128)(2,1)S(1)} %shard_map.47), channel_id=1, replica_groups=mesh['x'=4,'z'=16,'y'=4,'c'=2] {'x','z'}, dimensions={0} | all-to-all | bytes 262144 | tf_op jit(solution)/shard_map/all_to_all | solution.py:148
  75.8 0.0 copy-done.1
  75.8 0.0 copy-done.3
  75.8 0.0 copy-done.4
  75.8 3.5 %shard_map.48 = bf16[4,512,512]{2,1,0:T(8,128)(2,1)S(1)} custom-call(bf16[512,512]{1,0:T(8,128)(2,1)S(1)} %copy-done.4, bf16[512,512]{1,0:T(8,128)(2,1)S(1)} %copy-done.1, bf16[512,512]{1,0:T(8,128)(2,1)S(1)} %copy-done.3, bf16[512,128]{1,0:T(8,128)(2,1)S(1)} %bitcast.6), custom_call_target="tpu_custom_call" | custom-call | tf_op jit(solution)/shard_map/pallas_call | solution.py:149
  79.3 23.5 %all_to_all.23.own_ref = bf16[4,512,512]{2,1,0:T(8,128)(2,1)S(1)} all-to-all(bf16[4,512,512]{2,1,0:T(8,128)(2,1)S(1)} %shard_map.48), channel_id=1, replica_groups=mesh['x'=4,'z'=16,'y'=4,'c'=2] {'y'}, dimensions={0} | all-to-all | bytes 4194304 | tf_op jit(solution)/shard_map/all_to_all | solution.py:157
  102.8 8.7 %collective-permute-start.1 = (bf16[4,512,512]{2,1,0:T(8,128)(2,1)S(1)}, bf16[4,512,512]{2,1,0:T(8,128)(2,1)}, u32[]{:S(2)}, u32[]{:S(2)}) collective-permute-start(bf16[4,512,512]{2,1,0:T(8,128)(2,1)S(1)} %all_to_all.23.own_ref), channel_id=1, source_target_pairs={{0,1},{1,0},{2,3},{3,2},{4,5},{5,4},{6,7},{7,6},{8,9},{9,8},{10,11... | collective-permute-start | bytes 6291464 | tf_op jit(solution)/shard_map/ppermute | solution.py:158
  111.5 3.9 %collective-permute-done.1.far_ref = bf16[4,512,512]{2,1,0:T(8,128)(2,1)} collective-permute-done((bf16[4,512,512]{2,1,0:T(8,128)(2,1)S(1)}, bf16[4,512,512]{2,1,0:T(8,128)(2,1)}, u32[]{:S(2)}, u32[]{:S(2)}) %collective-permute-start.1) | collective-permute-done | bytes 2097184 | tf_op jit(solution)/shard_map/ppermute | solution.py:158
  115.4 0.3 all-gather.3.cloned.1.call-done
  115.7 4.6 %shard_map.49 = bf16[512,512]{1,0:T(8,128)(2,1)} custom-call(s32[1]{0:T(128)} %bitcast.core_ref, bf16[4,512,512]{2,1,0:T(8,128)(2,1)S(1)} %all_to_all.23.own_ref, bf16[4,512,512]{2,1,0:T(8,128)(2,1)} %collective-permute-done.1.far_ref, bf16[16,2,4,64,512]{4,3,2,1,0:T(8,128)(2,1)} %bitcast.7), custom_call_target="tpu_custom_call" | custom-call | tf_op jit(solution)/shard_map/pallas_call | solution.py:104
  (1 shorter events, 0.0 us)
Async XLA Ops:
  6.5 109.1 %all-gather.3.cloned.1.call-start = ((), (), s32[]{:S(2)}) async-start(), calls=%async_computation.4 | async-start | bytes 8650752 | tf_op jit(solution)/shard_map/all_gather | solution.py:142
  6.5 8.7 %collective-permute-start = (bf16[64,512]{1,0:T(8,128)(2,1)}, bf16[64,512]{1,0:T(8,128)(2,1)S(1)}, u32[]{:S(2)}, u32[]{:S(2)}) collective-permute-start(bf16[64,512]{1,0:T(8,128)(2,1)} %bitcast.8), channel_id=1, source_target_pairs={{0,256},{2,384},{4,0},{6,128},{128,258},{130,386},{132,2},{134,130... | collective-permute-start | bytes 196616 | tf_op jit(solution)/shard_map/ppermute | solution.py:127
  12.0 1.0 copy-start
  13.1 1.0 copy-start.2
  14.1 61.7 %copy-start.1 = (bf16[512,512]{1,0:T(8,128)(2,1)S(1)}, bf16[512,512]{1,0:T(8,128)(2,1)}, u32[]{:S(2)}) copy-start(bf16[512,512]{1,0:T(8,128)(2,1)} %k_ref.3) | copy-start | bytes 1572868
  14.1 61.7 %copy-start.3 = (bf16[512,512]{1,0:T(8,128)(2,1)S(1)}, bf16[512,512]{1,0:T(8,128)(2,1)}, u32[]{:S(2)}) copy-start(bf16[512,512]{1,0:T(8,128)(2,1)} %v_ref.3) | copy-start | bytes 1572868
  14.1 61.7 %copy-start.4 = (bf16[512,512]{1,0:T(8,128)(2,1)S(1)}, bf16[512,512]{1,0:T(8,128)(2,1)}, u32[]{:S(2)}) copy-start(bf16[512,512]{1,0:T(8,128)(2,1)} %q_ref.1) | copy-start | bytes 1572868
  102.8 12.6 %collective-permute-start.1 = (bf16[4,512,512]{2,1,0:T(8,128)(2,1)S(1)}, bf16[4,512,512]{2,1,0:T(8,128)(2,1)}, u32[]{:S(2)}, u32[]{:S(2)}) collective-permute-start(bf16[4,512,512]{2,1,0:T(8,128)(2,1)S(1)} %all_to_all.23.own_ref), channel_id=1, source_target_pairs={{0,1},{1,0},{2,3},{3,2},{4,5},{5,4},{6,7},{7,6},{8,9},{9,8},{10,11... | collective-permute-start | bytes 6291464 | tf_op jit(solution)/shard_map/ppermute | solution.py:158
Sparse Core Ops, SparseCore 0:
  25.9 89.7 all-gather.2
